TPU v7x, 32 devices: a whole 2x2x4 slice. The times are simulated.
32 devices in a mesh: groups: 2 (over x), gx: 8 (over z, y), gy: 2 (over core).
Axes of the slice: x: 2, y: 2, z: 4, core: 2. Of those that a mesh axis runs over, the one named last changes fastest.
Arguments:
- currents: bfloat16 [64, 8, 2, 128, 256], P(('groups', 'gx'), 'gy'), parts along dimension 0, may hold values from -6 to 6
- self_blocks: bfloat16 [64, 8, 2, 256, 256], P(('groups', 'gx'), 'gy'), parts along dimension 0, may hold values from -0.25 to 0.25
- near_blocks: bfloat16 [16, 2, 40, 2, 256, 256], P(('groups', 'gx'), 'gy'), parts along dimension 0, may hold values from -0.25 to 0.25
- near_pairs: int32 [16, 2, 40, 2], P(('groups', 'gx'), 'gy'), parts along dimension 0, may hold values from 0 to 15, as said below
- near_count: int32 [16, 2], P(('groups', 'gx'), 'gy'), parts along dimension 0, may hold values from 1 to 40, as said below
- basis: bfloat16 [64, 8, 2, 32, 256], P(('groups', 'gx'), 'gy'), parts along dimension 0, may hold values from -0.375 to 0.375
- transfer: bfloat16 [64, 8, 2, 1024], P(('groups', 'gx'), 'gy'), parts along dimension 0, may hold values from -0.75 to 0.75
- coupling: bfloat16 [128, 64, 2, 1024], P(('groups', 'gx', 'gy')), parts along dimension 0, may hold values from -0.09375 to 0.09375
- far_shift: int32 [128, 64, 2], P(('groups', 'gx', 'gy')), parts along dimension 0, may hold values from -1 to 1
- far_mask: int32 [128, 64], P(('groups', 'gx', 'gy')), parts along dimension 0, may hold values 0 or 1
- parent: int32 [64, 8], P(('groups', 'gx'), 'gy'), parts along dimension 0, may hold values from 0 to 63, as said below
- bloch: float32 [4], P('groups'), parts along dimension 0, may hold values from -3.140625 to 3.140625
Outputs:
- product: bfloat16 [64, 8, 2, 128, 256], P(('groups', 'gx'), 'gy'), parts along dimension 0
There are 2 independent parts, one for each index of `groups`. A program takes and returns all parts, laid end to end along the dimension named above; each array names one. Nothing has to cross between parts.
Inputs may be any that keep to these rules, and one draw needn't show every extreme that they name: `near_pairs`: column 0 is a block of the tile numbered i * 4 + j, column 1 a neighbour direction from 0 to 7; slots at or past the tile's live count hold entries of the same law. `near_count`: some tile holds exactly 40 live slots. A block of tile (tx, ty) has its parent among the 4 clusters from 4 * (tx * 2 + ty) on.
All inputs are finite; a program needn't handle non-finite values. No bound on the sum of `far_mask` on one device may be relied on, other than what follows from the above.
Results may differ from a plain program's by a relative error of at most 0.0042.
Values may be sent and summed in bfloat16 or wider, within the bound.
No kernel may reach another device: no remote copies, remote signals or barrier semaphores. Data moves between devices by JAX's collectives and lax.ppermute only.
A program may use at most 192 MiB of HBM per device.

v0:
```python
import functools

import jax
import jax.numpy as jnp
from jax import lax
from jax.experimental import pallas as pl
from jax.experimental.pallas import tpu as pltpu
from jax.sharding import PartitionSpec as P

F32 = jnp.float32
BF16 = jnp.bfloat16
GROUP = 4
DEPTH = 3
MIB = 1024 * 1024
VMEM_MIB = {"edges": 8, "leaf": 16, "outward": 54, "fold": 4, "itself": 16, "turn": 12, "near": 46, "far": 26, "last": 8}


def dot_nn(a, b):
    return lax.dot_general(a, b, (((1,), (0,)), ((), ())), preferred_element_type=F32)


def dot_nt(a, b):
    return lax.dot_general(a, b, (((1,), (1,)), ((), ())), preferred_element_type=F32)


def dot_tn(a, b):
    return lax.dot_general(a, b, (((0,), (0,)), ((), ())), preferred_element_type=F32)


def set_pair(win, at, re, im, half):
    panels = re.shape[1]
    win[at, :half, :panels] = re
    win[at, half:, :panels] = im
    win[at, :half, panels:] = -im
    win[at, half:, panels:] = re


def forward(pair, mats):
    return dot_nt(pair, jnp.concatenate([mats[0], mats[1]], axis=1))


def transposed(pair, mats):
    return dot_nn(pair, jnp.concatenate([mats[0], mats[1]], axis=0))


def turned(value, cos, sin, half):
    re = value[:half].astype(F32)
    im = value[half:].astype(F32)
    return cos * re - sin * im, sin * re + cos * im


def cell_phase(bloch, x, y, wide_x, wide_y, panels):
    shift_x = shift_y = 0.0
    if x == 0:
        shift_x = jnp.where(lax.axis_index("gx") == 0, -1.0, 0.0)
    if x == wide_x - 1:
        shift_x = jnp.where(lax.axis_index("gx") == lax.axis_size("gx") - 1, 1.0, 0.0)
    if y == 0:
        shift_y = jnp.where(lax.axis_index("gy") == 0, -1.0, 0.0)
    if y == wide_y - 1:
        shift_y = jnp.where(lax.axis_index("gy") == lax.axis_size("gy") - 1, 1.0, 0.0)
    phase = jnp.full((1, panels), bloch[0] * shift_x + bloch[1] * shift_y, F32)
    return jnp.cos(phase), jnp.sin(phase)


def slot_place(pairs, s, tile_y):
    r = pairs[0, s]
    d = pairs[1, s]
    u = d + jnp.where(d >= 4, 1, 0)
    ux = jnp.where(u >= 6, 2, jnp.where(u >= 3, 1, 0))
    rx = lax.div(r, tile_y)
    ry = r - rx * tile_y
    return r, rx + ux, ry + u - 3 * ux


def list_slots(pairs, count, lists, tile_x, tile_y):
    def one(s, found):
        _, cx, cy = slot_place(pairs, s, tile_y)
        outside = (cx == 0) | (cx == tile_x + 1) | (cy == 0) | (cy == tile_y + 1)
        lists[0, found[0]] = s
        lists[1, found[1]] = s
        step = jnp.where(outside, 1, 0)
        return found[0] + 1 - step, found[1] + step

    zero = jnp.int32(0)
    found = lax.fori_loop(0, count, one, (zero, zero))
    for k in range(2):
        lists[2, k] = found[k]
        for more in range(GROUP):
            lists[k, found[k] + more] = 0


def groups_of(n):
    return lax.div(n + GROUP - 1, GROUP)


def stream(groups, fetch, ring, sems, body):
    def start(g):
        @pl.when(g < groups)
        def _():
            at = lax.rem(g, DEPTH)
            for k in range(GROUP):
                fetch(g * GROUP + k, ring.at[at, k], sems.at[at, k])

    def prime():
        for g in range(DEPTH - 1):
            start(g)

    def step(g, carry):
        at = lax.rem(g, DEPTH)
        for k in range(GROUP):
            pltpu.make_async_copy(ring.at[at, k], ring.at[at, k], sems.at[at, k]).wait()
        start(g + DEPTH - 1)
        body(g, at)
        return carry

    return prime, lambda first, last: lax.fori_loop(first, last, step, 0)


def out_kernel(
    tile_x, tile_y, half, pairs, count, bloch, own, near, left, right, low_corner, high_corner, beside, lists, win, acc, ring,
    sems
):
    blocks = tile_x * tile_y
    wide_x, wide_y = tile_x + 2, tile_y + 2
    panels = own.shape[2]
    list_slots(pairs, count[0, 0], lists, tile_x, tile_y)
    n = lists[2, 1]
    groups = groups_of(n)

    def fetch(t, to, sem):
        pltpu.make_async_copy(near.at[lists[1, t]], to, sem).start()

    def body(g, at):
        for k in range(GROUP):
            t = g * GROUP + k
            r, cx, cy = slot_place(pairs, lists[1, t], tile_y)
            over = jnp.where(cx == 0, 0, wide_y) + cy
            along = 2 * wide_y + jnp.where(cy == 0, 0, tile_x) + cx - 1
            c = jnp.where((cx == 0) | (cx == wide_x - 1), over, along)
            acc[jnp.where(t < n, c, 2 * wide_y + 2 * tile_x)] += transposed(win[r], ring[at, k])

    prime, run = stream(groups, fetch, ring, sems, body)
    prime()
    for b in range(blocks):
        set_pair(win, b, own[b, :half], own[b, half:], half)
    acc[...] = jnp.zeros_like(acc)
    run(0, groups)
    for side in range(2):
        for cy in range(wide_y):
            cos, sin = cell_phase(bloch, (wide_x - 1) * side, cy, wide_x, wide_y, panels)
            re, im = turned(acc.at[side * wide_y + cy], cos, -sin, half)
            if 0 < cy < wide_y - 1:
                row = (left, right)[side]
                row[cy - 1, :half, :] = re.astype(BF16)
                row[cy - 1, half:, :] = im.astype(BF16)
            else:
                corner = (low_corner, high_corner)[side]
                corner[min(cy, 1), :half, :] = re.astype(BF16)
                corner[min(cy, 1), half:, :] = im.astype(BF16)
        for i in range(tile_x):
            cos, sin = cell_phase(bloch, i + 1, (wide_y - 1) * side, wide_x, wide_y, panels)
            re, im = turned(acc.at[2 * wide_y + side * tile_x + i], cos, -sin, half)
            beside[side, i, :half, :] = re.astype(BF16)
            beside[side, i, half:, :] = im.astype(BF16)


def fold_kernel(tile_y, low_corner, high_corner, unused_left, unused_right, left, right, ends, sems):
    del unused_left, unused_right
    steps = []
    for side, row, corner in ((0, left, low_corner), (1, right, high_corner)):
        for end, j in ((0, tile_y - 1), (1, 0)):
            k = 2 * side + end
            get = pltpu.make_async_copy(row.at[j], ends.at[k], sems.at[0, k])
            put = pltpu.make_async_copy(ends.at[k], row.at[j], sems.at[1, k])
            get.start()
            steps.append((get, put, k, corner, end))
    for get, put, k, corner, end in steps:
        get.wait()
        ends[k] = (ends[k].astype(F32) + corner[end].astype(F32)).astype(BF16)
        put.start()
    for _, put, _, _, _ in steps:
        put.wait()


def edge_kernel(tile_x, tile_y, own, first, last, columns, sems):
    blocks = tile_x * tile_y
    puts = [
        pltpu.make_async_copy(own.at[pl.ds(0, tile_y)], first, sems.at[0]),
        pltpu.make_async_copy(own.at[pl.ds(blocks - tile_y, tile_y)], last, sems.at[1]),
    ]
    for i in range(tile_x):
        for side in range(2):
            cell = own.at[i * tile_y + side * (tile_y - 1)]
            puts.append(pltpu.make_async_copy(cell, columns.at[side, i], sems.at[2 + 2 * i + side]))
    for put in puts:
        put.start()
    for put in puts:
        put.wait()


def turn_kernel(rank, bloch, shift, mask, mats, out, flat):
    lanes = flat.shape[1]
    sources = mats.shape[2]
    for p in range(mats.shape[0]):
        phase = bloch[0] * shift[p, 0:1, :].astype(F32) + bloch[1] * shift[p, 1:2, :].astype(F32)
        keep = mask[p : p + 1, :].astype(F32)
        cos, sin = keep * jnp.cos(phase), keep * jnp.sin(phase)
        both = jnp.concatenate([mats[p, 0], mats[p, 1]], axis=0).astype(F32).T
        turn = jnp.concatenate([both[:, sources:], both[:, :sources]], axis=1)
        both = jnp.concatenate([cos, cos], axis=1) * both + jnp.concatenate([-sin, sin], axis=1) * turn
        for at in range(0, 2 * sources, lanes):
            flat[...] = both[:, at : at + lanes]
            for l in range(rank):
                rows = flat[pl.ds(l, rank, stride=rank), :]
                out[l, p * rank : (p + 1) * rank, at : at + lanes] = rows.astype(BF16)


def leaf_kernel(blocks, rank, half, parent, own, basis, moves, unused, coeff, acc):
    del unused
    base = (lax.axis_index("gx") * lax.axis_size("gy") + lax.axis_index("gy")) * acc.shape[0]
    acc[...] = jnp.zeros_like(acc)
    for b in range(blocks):
        raw = dot_nt(basis[b], own[b])
        real = raw[:rank, :half] - raw[rank:, half:]
        imag = raw[:rank, half:] + raw[rank:, :half]
        leaf = jnp.concatenate([real, imag], axis=0)
        high = leaf.astype(BF16)
        low = (leaf - high.astype(F32)).astype(BF16)
        acc[parent[b // parent.shape[1], b % parent.shape[1]] - base] += dot_nn(moves[b], high) + dot_nn(moves[b], low)
    for q in range(acc.shape[0]):
        coeff[q * rank : (q + 1) * rank, :half] = acc[q, :rank].astype(BF16)
        coeff[q * rank : (q + 1) * rank, half:] = acc[q, rank:].astype(BF16)


def self_kernel(blocks, half, own, own_mats, total, win, ring, sems):
    groups = blocks // GROUP

    def fetch(t, to, sem):
        pltpu.make_async_copy(own_mats.at[t], to, sem).start()

    def body(g, at):
        for k in range(GROUP):
            t = g * GROUP + k
            set_pair(win, k, own[t, :half], own[t, half:], half)
        for k in range(GROUP):
            total[g * GROUP + k] = forward(win[k], ring[at, k])

    prime, run = stream(groups, fetch, ring, sems, body)
    prime()
    run(0, groups)


def near_kernel(
    tile_x, tile_y, half, pairs, lists, bloch, own, beside, from_left, from_right, corner, begun, near, total, win, ring, sems,
    begun_sem
):
    blocks = tile_x * tile_y
    wide_x, wide_y = tile_x + 2, tile_y + 2
    panels = own.shape[2]
    n, n_over = lists[2, 0], lists[2, 1]
    begin = pltpu.make_async_copy(begun, total.at[pl.ds(0, blocks)], begun_sem)
    begin.start()
    groups = groups_of(n)
    side_at, over_at = blocks, blocks + 2 * tile_x

    def slot(t):
        return jnp.where(t < groups * GROUP, lists[0, t], lists[1, jnp.maximum(t - groups * GROUP, 0)])

    def fetch(t, to, sem):
        pltpu.make_async_copy(near.at[slot(t)], to, sem).start()

    def body(g, at):
        @pl.when(g < groups)
        def _():
            for k in range(GROUP):
                t = g * GROUP + k
                r, cx, cy = slot_place(pairs, lists[0, t], tile_y)
                live = t < n
                r = jnp.where(live, r, 0)
                c = jnp.where(live, (cx - 1) * tile_y + cy - 1, 0)
                total[jnp.where(live, r, blocks)] += forward(win[c], ring[at, k])
                total[jnp.where(live, c, blocks)] += transposed(win[r], ring[at, k])

        @pl.when(g >= groups)
        def _():
            for k in range(GROUP):
                t = (g - groups) * GROUP + k
                r, cx, cy = slot_place(pairs, lists[1, t], tile_y)
                live = t < n_over
                over = over_at + jnp.where(cx == 0, 0, wide_y) + cy
                c = jnp.where((cx == 0) | (cx == wide_x - 1), over, side_at + jnp.where(cy == 0, 0, tile_x) + cx - 1)
                total[jnp.where(live, r, blocks)] += forward(win[jnp.where(live, c, 0)], ring[at, k])

    every_group = groups + groups_of(n_over)
    prime, run = stream(every_group, fetch, ring, sems, body)
    prime()
    for b in range(blocks):
        set_pair(win, b, own[b, :half], own[b, half:], half)
    for side in range(2):
        for i in range(tile_x):
            cos, sin = cell_phase(bloch, i + 1, side * (wide_y - 1), wide_x, wide_y, panels)
            re, im = turned(beside.at[1 - side, i], cos, sin, half)
            set_pair(win, side_at + side * tile_x + i, re.astype(BF16), im.astype(BF16), half)
        for cy in range(wide_y):
            if cy == 0:
                cell = corner.at[2 * side + 1]
            elif cy == wide_y - 1:
                cell = corner.at[2 * side]
            else:
                cell = (from_left, from_right)[side].at[cy - 1]
            cos, sin = cell_phase(bloch, (wide_x - 1) * side, cy, wide_x, wide_y, panels)
            re, im = turned(cell, cos, sin, half)
            set_pair(win, over_at + side * wide_y + cy, re.astype(BF16), im.astype(BF16), half)
    begin.wait()
    run(0, every_group)


def far_kernel(
    tile_x, tile_y, half, rank, parent, back, coeff, other_low, other_high, coupling, moves, basis, near_total, out, edge, far, gathered,
    stage, out_sem
):
    blocks = tile_x * tile_y
    gx_index, gy_index = lax.axis_index("gx"), lax.axis_index("gy")
    base = (gx_index * lax.axis_size("gy") + gy_index) * far.shape[0]
    rows = far.shape[0] * rank
    middle = coeff.shape[0] // rows // 2
    for first, source, core in ((0, coeff, gy_index), (0, other_low, 1 - gy_index), (middle, other_high, 1 - gy_index)):
        for k in range(first, first + source.shape[0] // rows):
            tile = k * 2 + core
            at = pl.multiple_of(tile * rows, rows)
            for plane in range(2):
                piece = source[(k - first) * rows : (k - first + 1) * rows, plane * half : (plane + 1) * half]
                gathered[plane, pl.ds(at, rows), :] = piece.astype(F32)
    every = gathered.shape[1] // rank
    reals, imags = gathered.at[0], gathered.at[1]
    raw = jnp.zeros((coupling.shape[1], 2 * half), F32)
    for l in range(0, rank, 2):
        terms = []
        for m in (l, l + 1):
            re = reals[pl.ds(m, every, stride=rank), :]
            im = imags[pl.ds(m, every, stride=rank), :]
            terms.append(jnp.concatenate([re, im], axis=1).astype(BF16))
            terms.append(jnp.concatenate([-im, re], axis=1).astype(BF16))
        raw = raw + dot_nn(jnp.concatenate([coupling[l], coupling[l + 1]], axis=1), jnp.concatenate(terms, axis=0))
    for p in range(far.shape[0]):
        far[p, :rank, :] = raw[rank * p : rank * (p + 1), :half]
        far[p, rank:, :] = -raw[rank * p : rank * (p + 1), half:]

    def block(b):
        chosen_far = far[parent[b // tile_y, b % tile_y] - base]
        high = chosen_far.astype(BF16)
        low = (chosen_far - high.astype(F32)).astype(BF16)
        down = (dot_tn(moves[b], high) + dot_tn(moves[b], low)).astype(BF16)
        both = jnp.concatenate([down, jnp.concatenate([-down[rank:], down[:rank]], axis=0)], axis=1)
        value = dot_tn(both, basis[b]) + near_total[b]
        j = b % tile_y
        if j == tile_y - 1:
            value = value + back[0, b // tile_y].astype(F32)
        if j == 0:
            value = value + back[1, b // tile_y].astype(F32)
        return value

    inner = (tile_x - 2) * tile_y
    for b in range(tile_y, blocks - tile_y):
        stage[b - tile_y] = block(b).astype(BF16)
    put = pltpu.make_async_copy(stage, out.at[pl.ds(tile_y, inner)], out_sem)
    put.start()
    for j in range(tile_y):
        edge[j] = block(j)
        edge[tile_y + j] = block(blocks - tile_y + j)
    put.wait()


def last_kernel(tile_x, tile_y, edge, to_first, to_last, unused, out, stage, sems):
    del unused
    blocks = tile_x * tile_y
    puts = []
    for side, came in ((0, to_first), (1, to_last)):
        for j in range(tile_y):
            c = side * tile_y + j
            stage[c] = (edge[c] + came[j].astype(F32)).astype(BF16)
            put = pltpu.make_async_copy(stage.at[c], out.at[j + side * (blocks - tile_y)], sems.at[c])
            put.start()
            puts.append(put)
    for put in puts:
        put.wait()


SMEM = pl.BlockSpec(memory_space=pltpu.SMEM)
VMEM = pl.BlockSpec(memory_space=pltpu.VMEM)
ANY = pl.BlockSpec(memory_space=pl.ANY)


def call(kernel, ins, in_specs, outs, out_specs, scratch, flops, moved, name, aliases=None):
    return pl.pallas_call(
        kernel,
        out_shape=outs,
        in_specs=in_specs,
        out_specs=out_specs,
        scratch_shapes=scratch,
        input_output_aliases=aliases or {},
        compiler_params=pltpu.CompilerParams(vmem_limit_bytes=VMEM_MIB[name] * MIB),
        cost_estimate=pl.CostEstimate(flops=flops // 100, bytes_accessed=moved // 100, transcendentals=0),
        name=name,
    )(*ins)


def per_device(
    currents, self_blocks, near_blocks, near_pairs, near_count, basis, transfer, coupling, far_shift, far_mask, parent, bloch
):
    tile_x, tile_y, _, half, panels = currents.shape
    rank = basis.shape[3]
    blocks = tile_x * tile_y
    wide_x, wide_y = tile_x + 2, tile_y + 2
    gx_count, gy_count = lax.axis_size("gx"), lax.axis_size("gy")
    gx_index, gy_index = lax.axis_index("gx"), lax.axis_index("gy")
    clusters = far_mask.shape[0]
    tiles = gx_count * gy_count
    width = 2 * half
    slots = near_pairs.shape[2]

    def shape(*dims, dtype=BF16):
        return jax.ShapeDtypeStruct(dims, dtype)

    right = [(i, (i + 1) % gx_count) for i in range(gx_count)]
    left = [((i + 1) % gx_count, i) for i in range(gx_count)]
    swap = [(i, (i + 1) % gy_count) for i in range(gy_count)]

    own = currents.reshape(blocks, width, panels)
    pairs = near_pairs.reshape(slots, 2).T
    first, last, columns = call(
        functools.partial(edge_kernel, tile_x, tile_y),
        (own,),
        [VMEM],
        [shape(tile_y, width, panels), shape(tile_y, width, panels), shape(2, tile_x, width, panels)],
        [ANY] * 3,
        [pltpu.SemaphoreType.DMA((2 + 2 * tile_x,))],
        0,
        0,
        "edges",
    )
    from_left = lax.ppermute(last, "gx", right)
    from_right = lax.ppermute(first, "gx", left)
    beside = lax.ppermute(columns, "gy", swap)

    near = near_blocks.reshape(slots, 2, panels, panels)
    own_mats = self_blocks.reshape(blocks, 2, panels, panels)
    basis_b = basis.reshape(blocks, 2 * rank, panels)
    tr = transfer.reshape(blocks, 2, rank, rank)
    moves = jnp.concatenate(
        [jnp.concatenate([tr[:, 0], -tr[:, 1]], axis=2), jnp.concatenate([tr[:, 1], tr[:, 0]], axis=2)], axis=1
    )

    back_left, back_right, low_corner, high_corner, beside_out, lists = call(
        functools.partial(out_kernel, tile_x, tile_y, half),
        (pairs, near_count, bloch, own, near),
        [SMEM, SMEM, SMEM, VMEM, ANY],
        [
            shape(tile_y, width, panels),
            shape(tile_y, width, panels),
            shape(2, width, panels),
            shape(2, width, panels),
            shape(2, tile_x, width, panels),
            shape(3, slots + 2 * GROUP, dtype=jnp.int32),
        ],
        [VMEM] * 5 + [SMEM],
        [
            pltpu.VMEM((blocks, width, 2 * panels), BF16),
            pltpu.VMEM((2 * wide_y + 2 * tile_x + 1, width, panels), F32),
            pltpu.VMEM((DEPTH, GROUP, 2, panels, panels), BF16),
            pltpu.SemaphoreType.DMA((DEPTH, GROUP)),
        ],
        2 * 10 * 2 * width * panels * panels,
        own.size * 2 + 10 * 2 * 2 * panels * panels,
        "outward",
    )
    low_corner = lax.ppermute(low_corner, "gy", swap)
    high_corner = lax.ppermute(high_corner, "gy", swap)
    back = lax.ppermute(beside_out, "gy", swap)
    coeff = call(
        functools.partial(leaf_kernel, blocks, rank, half),
        (parent, own, basis_b, moves, first),
        [SMEM, VMEM, VMEM, VMEM, ANY],
        shape(clusters * rank, width),
        VMEM,
        [pltpu.VMEM((clusters, 2 * rank, half), F32)],
        2 * blocks * 2 * rank * panels * width,
        own.size * 2 + basis_b.size * 2,
        "leaf",
    )
    back_left, back_right = call(
        functools.partial(fold_kernel, tile_y),
        (low_corner, high_corner, back_left, back_right),
        [VMEM, VMEM, ANY, ANY],
        [shape(tile_y, width, panels), shape(tile_y, width, panels)],
        [ANY, ANY],
        [pltpu.VMEM((4, width, panels), BF16), pltpu.SemaphoreType.DMA((2, 4))],
        0,
        0,
        "fold",
        aliases={2: 0, 3: 1},
    )
    to_last = lax.ppermute(back_left, "gx", left)
    to_first = lax.ppermute(back_right, "gx", right)

    self_total = call(
        functools.partial(self_kernel, blocks, half),
        (own, own_mats),
        [VMEM, ANY],
        shape(blocks, width, panels, dtype=F32),
        VMEM,
        [
            pltpu.VMEM((GROUP, width, 2 * panels), BF16),
            pltpu.VMEM((DEPTH, GROUP, 2, panels, panels), BF16),
            pltpu.SemaphoreType.DMA((DEPTH, GROUP)),
        ],
        0,
        0,
        "itself",
    )
    coeff = lax.all_to_all(jnp.broadcast_to(coeff[None], (gx_count,) + coeff.shape), "gx", 0, 0).reshape(-1, width)
    mats = coupling.transpose(0, 2, 1, 3)
    sources = 2 * mats.shape[2]
    mats = call(
        functools.partial(turn_kernel, rank),
        (bloch, far_shift.transpose(0, 2, 1), far_mask, mats),
        [SMEM, VMEM, VMEM, VMEM],
        shape(rank, clusters * rank, sources),
        VMEM,
        [pltpu.VMEM((rank * rank, min(sources, 128)), F32)],
        0,
        0,
        "turn",
    )

    from_left, from_right, _ = lax.optimization_barrier((from_left, from_right, self_total))
    halo_corner = jnp.stack([from_left[0], from_left[tile_y - 1], from_right[0], from_right[tile_y - 1]])
    halo_corner = lax.ppermute(halo_corner, "gy", swap)
    near_total = call(
        functools.partial(near_kernel, tile_x, tile_y, half),
        (pairs, lists, bloch, own, beside, from_left, from_right, halo_corner, self_total, near),
        [SMEM] * 3 + [VMEM] * 5 + [ANY, ANY],
        shape(blocks + 1, width, panels, dtype=F32),
        VMEM,
        [
            pltpu.VMEM((blocks + 2 * tile_x + 2 * wide_y, width, 2 * panels), BF16),
            pltpu.VMEM((DEPTH, GROUP, 2, panels, panels), BF16),
            pltpu.SemaphoreType.DMA((DEPTH, GROUP)),
            pltpu.SemaphoreType.DMA,
        ],
        0,
        0,
        "near",
    )
    coeff, near_total = lax.optimization_barrier((coeff, near_total))
    middle = coeff.shape[0] // 2
    other_low = lax.ppermute(coeff[:middle], "gy", swap)
    other_high = lax.ppermute(coeff[middle:], "gy", swap)

    out, edge = call(
        functools.partial(far_kernel, tile_x, tile_y, half, rank),
        (parent, back, coeff, other_low, other_high, mats, moves, basis_b, near_total),
        [SMEM] + [VMEM] * 8,
        [shape(blocks, width, panels), shape(2 * tile_y, width, panels, dtype=F32)],
        [ANY, VMEM],
        [
            pltpu.VMEM((clusters, 2 * rank, half), F32),
            pltpu.VMEM((2, clusters * tiles * rank, half), F32),
            pltpu.VMEM(((tile_x - 2) * tile_y, width, panels), BF16),
            pltpu.SemaphoreType.DMA,
        ],
        0,
        0,
        "far",
    )
    cells = (2 * tile_y, width, panels)
    out = call(
        functools.partial(last_kernel, tile_x, tile_y),
        (edge, to_first, to_last, out),
        [VMEM, VMEM, VMEM, ANY],
        shape(blocks, width, panels),
        ANY,
        [pltpu.VMEM(cells, BF16), pltpu.SemaphoreType.DMA((2 * tile_y,))],
        0,
        0,
        "last",
        aliases={3: 0},
    )
    return out.reshape(currents.shape)


def solution(mesh):
    placed = (
        P(("groups", "gx"), "gy", None, None, None),
        P(("groups", "gx"), "gy", None, None, None),
        P(("groups", "gx"), "gy", None, None, None, None),
        P(("groups", "gx"), "gy", None, None),
        P(("groups", "gx"), "gy"),
        P(("groups", "gx"), "gy", None, None, None),
        P(("groups", "gx"), "gy", None, None),
        P(("groups", "gx", "gy"), None, None, None),
        P(("groups", "gx", "gy"), None, None),
        P(("groups", "gx", "gy"), None),
        P(("groups", "gx"), "gy"),
        P("groups"),
    )
    return jax.shard_map(
        per_device,
        mesh=mesh,
        in_specs=placed,
        out_specs=P(("groups", "gx"), "gy", None, None, None),
        check_vma=False,
    )
```

profile of v0, /device:TPU:0, one launch (start us, length us, event | category | flops | bytes accessed | tf_op | source)
XLA Modules:
  0.0 72.3 jit_solution(270953538143754132)
XLA Ops:
  0.0 1.6 %copy-done = bf16[4,4,2,128,256]{4,3,2,1,0:T(8,128)(2,1)S(1)} copy-done((bf16[4,4,2,128,256]{4,3,2,1,0:T(8,128)(2,1)S(1)}, bf16[4,4,2,128,256]{4,3,2,1,0:T(8,128)(2,1)}, u32[]{:S(2)}) %copy-start) | copy-done | bytes 2097176
  1.6 1.4 %edges.1 = (bf16[4,256,256]{2,1,0:T(8,128)(2,1)}, bf16[4,256,256]{2,1,0:T(8,128)(2,1)}, bf16[2,4,256,256]{3,2,1,0:T(8,128)(2,1)}) custom-call(bf16[16,256,256]{2,1,0:T(8,128)(2,1)S(1)} %bitcast.22), custom_call_target="tpu_custom_call" | custom-call | tf_op jit(solution)/shard_map/edges/pallas_call | solution.py:396
  3.0 6.1 %collective-permute-start.3 = (bf16[4,256,256]{2,1,0:T(8,128)(2,1)}, bf16[4,256,256]{2,1,0:T(8,128)(2,1)S(1)}, u32[]{:S(2)}, u32[]{:S(2)}) collective-permute-start(bf16[4,256,256]{2,1,0:T(8,128)(2,1)} %get-tuple-element.23.unused), channel_id=1, source_target_pairs={{2,0},{4,2},{6,4},{8,6},{10,8},{12,10},{14,12},{0,14},{3,1},{5,3},... | collective-permute-start | bytes 1572872 | tf_op jit(solution)/shard_map/ppermute | solution.py:444
  9.1 0.9 %copy.16 = bf16[4,4,2,1024]{3,1,0,2:T(4,128)(2,1)S(1)} copy(bf16[4,4,2,1024]{3,2,1,0:T(2,128)(2,1)} %param.18) | data formatting | bytes 131072 | tf_op args[6]
  9.9 0.2 reshape.29
  10.2 0.2 maximum_maximum_fusion.moves
  10.4 0.0 copy-start.7
  10.4 0.7 copy-done.7
  11.1 3.2 %leaf.1 = bf16[128,256]{1,0:T(8,128)(2,1)S(1)} custom-call(s32[4,4]{1,0:T(4,128)S(1)} %copy-done.7, bf16[16,256,256]{2,1,0:T(8,128)(2,1)S(1)} %bitcast.23, bf16[16,64,256]{2,1,0:T(8,128)(2,1)S(1)} %bitcast.30, bf16[16,64,64]{2,1,0:T(8,128)(2,1)S(1)} %maximum_maximum_fusion.moves, bf16[4,256,256]{2,1,0:T(8,128)(2,1)} %get-tuple-element.23.unused), custom_call_target="tpu_custom_call" | custom-call | flops 1342177 | bytes 26214 | tf_op jit(solution)/shard_map/leaf/pallas_call | solution.py:396
  14.2 0.8 %broadcast_in_dim.2 = bf16[8,128,256]{2,1,0:T(8,128)(2,1)} broadcast(bf16[128,256]{1,0:T(8,128)(2,1)S(1)} %leaf.1), dimensions={1,2} | broadcast | bytes 589824 | tf_op jit(solution)/shard_map/broadcast_in_dim | solution.py:522
  15.1 6.0 %all-to-all-start = ((bf16[8,128,256]{2,1,0:T(8,128)(2,1)}), bf16[8,128,256]{2,1,0:T(8,128)(2,1)S(1)}, u32[]{:S(2)}, u32[]{:S(2)}) async-start(bf16[8,128,256]{2,1,0:T(8,128)(2,1)} %broadcast_in_dim.2), calls=%async_computation | async-start | bytes 1048576 | tf_op jit(solution)/shard_map/all_to_all | solution.py:522
  21.8 7.3 %outward.1 = (bf16[4,256,256]{2,1,0:T(8,128)(2,1)}, bf16[4,256,256]{2,1,0:T(8,128)(2,1)}, bf16[2,256,256]{2,1,0:T(8,128)(2,1)}, bf16[2,256,256]{2,1,0:T(8,128)(2...) custom-call(s32[2,40]{1,0:T(2,128)} %bitcast.33, s32[1,1]{1,0:T(1,128)S(6)} %copy.23.count, f32[2]{0:T(128)} %bloch.5, ...), custom_call_target="tpu_custom_call" | custom-call | flops 6710886 | bytes 47185 | tf_op jit(solution)/shard_map/outward/pallas_call | solution.py:396
  29.1 0.1 collective-permute-start
  29.3 2.4 %itself.1.begun = f32[16,256,256]{2,1,0:T(8,128)S(1)} custom-call(bf16[16,256,256]{2,1,0:T(8,128)(2,1)S(1)} %bitcast.24, bf16[16,2,256,256]{3,2,1,0:T(8,128)(2,1)S(1)} %bitcast.28), custom_call_target="tpu_custom_call" | custom-call | tf_op jit(solution)/shard_map/itself/pallas_call | solution.py:396
  31.6 2.0 %copy-done.4 = f32[16,256,256]{2,1,0:T(8,128)} copy-done((f32[16,256,256]{2,1,0:T(8,128)}, f32[16,256,256]{2,1,0:T(8,128)S(1)}, u32[]{:S(2)}) %copy-start.4) | copy-done | bytes 4194328
  33.6 0.5 collective-permute-done.3.from_right
  34.1 1.0 %fusion.2 = (bf16[1,256,256]{2,1,0:T(8,128)(2,1)S(1)}, bf16[1,256,256]{2,1,0:T(8,128)(2,1)S(1)}, bf16[1,256,256]{2,1,0:T(8,128)(2,1)S(1)}, bf16[1,256,256]{2,1,0:T(8,128)(2,1)S(1)}) fusion(bf16[4,256,256]{2,1,0:T(8,128)(2,1)} %collective-permute-done.2.from_left, bf16[4,256,256]{2,1,0:T(8,128)(2,1)S(1)} %collective-permute-done.3.from_right), kind=kLoop, calls=%fused_computation.7 | loop fusion | bytes 1048576 | tf_op jit(solution)/shard_map/slice | solution.py:538
  35.1 0.1 pad_maximum_fusion
  35.2 0.1 collective-permute-start.4
  35.3 0.5 collective-permute-start.7
  35.8 0.1 collective-permute-start.8
  35.8 1.7 %collective-permute-done.7.low_corner = bf16[2,256,256]{2,1,0:T(8,128)(2,1)S(1)} collective-permute-done((bf16[2,256,256]{2,1,0:T(8,128)(2,1)S(1)}, bf16[2,256,256]{2,1,0:T(8,128)(2,1)S(1)}, u32[]{:S(2)}, u32[]{:S(2)}) %collective-permute-start.7) | collective-permute-done | bytes 262176 | tf_op jit(solution)/shard_map/ppermute | solution.py:478
  37.5 0.4 collective-permute-done.8.high_corner
  37.9 1.8 %fold.1 = (bf16[4,256,256]{2,1,0:T(8,128)(2,1)}, bf16[4,256,256]{2,1,0:T(8,128)(2,1)}) custom-call(bf16[2,256,256]{2,1,0:T(8,128)(2,1)S(1)} %collective-permute-done.7.low_corner, bf16[2,256,256]{2,1,0:T(8,128)(2,1)S(1)} %collective-permute-done.8.high_corner, ...), custom_call_target="tpu_custom_call", output_to_operand_aliasing={{0}: (2, {}), {1}: (3, {})} | custom-call | tf_op jit(solution)/shard_map/fold/pallas_call | solution.py:396
  39.8 5.4 %collective-permute-start.10 = (bf16[4,256,256]{2,1,0:T(8,128)(2,1)}, bf16[4,256,256]{2,1,0:T(8,128)(2,1)S(1)}, u32[]{:S(2)}, u32[]{:S(2)}) collective-permute-start(bf16[4,256,256]{2,1,0:T(8,128)(2,1)} %get-tuple-element.37), channel_id=1, source_target_pairs={{2,0},{4,2},{6,4},{8,6},{10,8},{12,10},{14,12},{0,14},{3,1},{5,3},... | collective-permute-start | bytes 1572872 | tf_op jit(solution)/shard_map/ppermute | solution.py:504
  45.2 13.0 %near.1.near_total = f32[17,256,256]{2,1,0:T(8,128)} custom-call(s32[2,40]{1,0:T(2,128)S(1)} %bitcast.34, s32[3,48]{1,0:T(4,128)S(1)} %copy-done.12, f32[2]{0:T(128)S(1)} %copy-done.9, bf16[16,256,256]{2,1,0:T(8,128)(2,1)S(1)} %bitcast.25, bf16[2,4,256,256]{3,2,1,0:T(8,128)(2,1)} %collective-permute-done.1.beside, ...), custom_call_target="tpu_custom_call" | custom-call | tf_op jit(solution)/shard_map/near/pallas_call | solution.py:396
  58.3 0.1 collective-permute-start.5
  58.4 0.5 collective-permute-start.6
  58.9 1.8 %copy.19 = bf16[4,64,2,1024]{3,1,2,0:T(8,128)(2,1)S(1)} copy(bf16[4,64,2,1024]{3,2,1,0:T(2,128)(2,1)} %param.19) | data formatting | bytes 2097152 | tf_op args[7]
  60.7 3.0 %turn.1.coupling = bf16[32,128,128]{2,1,0:T(8,128)(2,1)S(1)} custom-call(f32[2]{0:T(128)S(1)} %copy-done.9, s32[4,2,64]{2,1,0:T(2,128)S(1)} %bitcast.32, s32[4,64]{1,0:T(4,128)S(1)} %copy-done.13, bf16[4,2,64,1024]{3,2,1,0:T(8,128)(2,1)S(1)} %bitcast.29), custom_call_target="tpu_custom_call" | custom-call | tf_op jit(solution)/shard_map/turn/pallas_call | solution.py:396
  63.7 6.3 %far.1 = (bf16[16,256,256]{2,1,0:T(8,128)(2,1)}, f32[8,256,256]{2,1,0:T(8,128)S(1)}) custom-call(s32[4,4]{1,0:T(4,128)S(1)} %copy-done.8, bf16[2,4,256,256]{3,2,1,0:T(8,128)(2,1)S(1)} %collective-permute-done.back, bf16[1024,256]{1,0:T(8,128)(2,1)S(1)} %bitcast.27, bf16[512,256]{1,0:T(8,128)(2,1)S(1)} %collective-permute-done.5.other_low, ...), custom_call_target="tpu_custom_call" | custom-call | tf_op jit(solution)/shard_map/far/pallas_call | solution.py:396
  70.0 2.1 %last.1 = bf16[16,256,256]{2,1,0:T(8,128)(2,1)} custom-call(f32[8,256,256]{2,1,0:T(8,128)S(1)} %get-tuple-element.31.edge, bf16[4,256,256]{2,1,0:T(8,128)(2,1)} %collective-permute-done.9.to_first, bf16[4,256,256]{2,1,0:T(8,128)(2,1)S(1)} %collective-permute-done.10.to_last, ...), custom_call_target="tpu_custom_call", output_to_operand_aliasing={{}: (3, {})} | custom-call | tf_op jit(solution)/shard_map/last/pallas_call | solution.py:396
  (43 shorter events, 0.2 us)
Async XLA Ops:
  0.0 1.6 %copy-start = (bf16[4,4,2,128,256]{4,3,2,1,0:T(8,128)(2,1)S(1)}, bf16[4,4,2,128,256]{4,3,2,1,0:T(8,128)(2,1)}, u32[]{:S(2)}) copy-start(bf16[4,4,2,128,256]{4,3,2,1,0:T(8,128)(2,1)} %param.12) | copy-start | bytes 6291460
  1.6 8.8 %copy-start.1 = (bf16[4,4,2,128,256]{4,3,2,1,0:T(8,128)(2,1)S(1)}, bf16[4,4,2,128,256]{4,3,2,1,0:T(8,128)(2,1)}, u32[]{:S(2)}) copy-start(bf16[4,4,2,128,256]{4,3,2,1,0:T(8,128)(2,1)} %param.12) | copy-start | bytes 6291460
  1.6 8.8 %copy-start.6 = (bf16[4,4,2,32,256]{4,3,2,1,0:T(8,128)(2,1)S(1)}, bf16[4,4,2,32,256]{4,3,2,1,0:T(8,128)(2,1)}, u32[]{:S(2)}) copy-start(bf16[4,4,2,32,256]{4,3,2,1,0:T(8,128)(2,1)} %param.17) | copy-start | bytes 1572868
  3.0 31.1 %collective-permute-start.3 = (bf16[4,256,256]{2,1,0:T(8,128)(2,1)}, bf16[4,256,256]{2,1,0:T(8,128)(2,1)S(1)}, u32[]{:S(2)}, u32[]{:S(2)}) collective-permute-start(bf16[4,256,256]{2,1,0:T(8,128)(2,1)} %get-tuple-element.23.unused), channel_id=1, source_target_pairs={{2,0},{4,2},{6,4},{8,6},{10,8},{12,10},{14,12},{0,14},{3,1},{5,3},... | collective-permute-start | bytes 1572872 | tf_op jit(solution)/shard_map/ppermute | solution.py:444
  9.1 25.0 %collective-permute-start.2 = (bf16[4,256,256]{2,1,0:T(8,128)(2,1)}, bf16[4,256,256]{2,1,0:T(8,128)(2,1)}, u32[]{:S(2)}, u32[]{:S(2)}) collective-permute-start(bf16[4,256,256]{2,1,0:T(8,128)(2,1)} %get-tuple-element.26), channel_id=1, source_target_pairs={{0,2},{2,4},{4,6},{6,8},{8,10},{10,12},{12,14},{14,0},{1,3},{3,5},... | collective-permute-start | bytes 1572872 | tf_op jit(solution)/shard_map/ppermute | solution.py:443
  9.1 36.1 %collective-permute-start.1 = (bf16[2,4,256,256]{3,2,1,0:T(8,128)(2,1)}, bf16[2,4,256,256]{3,2,1,0:T(8,128)(2,1)}, u32[]{:S(2)}, u32[]{:S(2)}) collective-permute-start(bf16[2,4,256,256]{3,2,1,0:T(8,128)(2,1)} %get-tuple-element.25), channel_id=1, source_target_pairs={{0,1},{1,0},{2,3},{3,2},{4,5},{5,4},{6,7},{7,6},{8,9},{9,8},{10,11... | collective-permute-start | bytes 3145736 | tf_op jit(solution)/shard_map/ppermute | solution.py:445
  10.4 0.7 copy-start.7
  15.1 43.1 %all-to-all-start = ((bf16[8,128,256]{2,1,0:T(8,128)(2,1)}), bf16[8,128,256]{2,1,0:T(8,128)(2,1)S(1)}, u32[]{:S(2)}, u32[]{:S(2)}) async-start(bf16[8,128,256]{2,1,0:T(8,128)(2,1)} %broadcast_in_dim.2), calls=%async_computation | async-start | bytes 1048576 | tf_op jit(solution)/shard_map/all_to_all | solution.py:522
  21.7 7.5 %copy-start.2 = (bf16[4,4,2,128,256]{4,3,2,1,0:T(8,128)(2,1)S(1)}, bf16[4,4,2,128,256]{4,3,2,1,0:T(8,128)(2,1)}, u32[]{:S(2)}) copy-start(bf16[4,4,2,128,256]{4,3,2,1,0:T(8,128)(2,1)} %param.12) | copy-start | bytes 6291460
  21.7 7.4 %copy-start.5 = (bf16[4,4,2,256,256]{4,3,2,1,0:T(8,128)(2,1)S(1)}, bf16[4,4,2,256,256]{4,3,2,1,0:T(8,128)(2,1)}, u32[]{:S(2)}) copy-start(bf16[4,4,2,256,256]{4,3,2,1,0:T(8,128)(2,1)} %param.13) | copy-start | bytes 12582916
  29.1 34.6 %collective-permute-start = (bf16[2,4,256,256]{3,2,1,0:T(8,128)(2,1)}, bf16[2,4,256,256]{3,2,1,0:T(8,128)(2,1)S(1)}, u32[]{:S(2)}, u32[]{:S(2)}) collective-permute-start(bf16[2,4,256,256]{3,2,1,0:T(8,128)(2,1)} %get-tuple-element.22), channel_id=1, source_target_pairs={{0,1},{1,0},{2,3},{3,2},{4,5},{5,4},{6,7},{7,6},{8,9},{9,8},{10,11... | collective-permute-start | bytes 3145736 | tf_op jit(solution)/shard_map/ppermute | solution.py:480
  29.2 6.1 %copy-start.15 = (bf16[2,256,256]{2,1,0:T(8,128)(2,1)S(1)}, bf16[2,256,256]{2,1,0:T(8,128)(2,1)}, u32[]{:S(2)}) copy-start(bf16[2,256,256]{2,1,0:T(8,128)(2,1)} %get-tuple-element.32) | copy-start | bytes 786436
  29.2 6.5 %copy-start.14 = (bf16[2,256,256]{2,1,0:T(8,128)(2,1)S(1)}, bf16[2,256,256]{2,1,0:T(8,128)(2,1)}, u32[]{:S(2)}) copy-start(bf16[2,256,256]{2,1,0:T(8,128)(2,1)} %get-tuple-element.33) | copy-start | bytes 786436
  29.2 15.9 %copy-start.9 = (f32[2]{0:T(128)S(1)}, f32[2]{0:T(128)}, u32[]{:S(2)}) copy-start(f32[2]{0:T(128)} %bloch.5) | copy-start | bytes 28
  29.2 15.9 %copy-start.11 = (s32[1,1,40,2]{2,3,1,0:T(2,128)S(1)}, s32[1,1,40,2]{2,3,1,0:T(2,128)}, u32[]{:S(2)}) copy-start(s32[1,1,40,2]{2,3,1,0:T(2,128)} %param.15) | copy-start | bytes 964
  29.2 15.9 %copy-start.12 = (s32[3,48]{1,0:T(4,128)S(1)}, s32[3,48]{1,0:T(4,128)}, u32[]{:S(2)}) copy-start(s32[3,48]{1,0:T(4,128)} %get-tuple-element.24.lists) | copy-start | bytes 1732
  31.6 2.0 %copy-start.4 = (f32[16,256,256]{2,1,0:T(8,128)}, f32[16,256,256]{2,1,0:T(8,128)S(1)}, u32[]{:S(2)}) copy-start(f32[16,256,256]{2,1,0:T(8,128)S(1)} %itself.1.begun) | copy-start | bytes 12582916
  35.2 10.0 %collective-permute-start.4 = (bf16[4,256,256]{2,1,0:T(8,128)(2,1)S(1)}, bf16[4,256,256]{2,1,0:T(8,128)(2,1)S(1)}, u32[]{:S(2)}, u32[]{:S(2)}) collective-permute-start(bf16[4,256,256]{2,1,0:T(8,128)(2,1)S(1)} %pad_maximum_fusion), channel_id=1, source_target_pairs={{0,1},{1,0},{2,3},{3,2},{4,5},{5,4},{6,7},{7,6},{8,9},{9,8},{10,11... | collective-permute-start | bytes 1572872 | tf_op jit(solution)/shard_map/ppermute | solution.py:539
  35.3 2.3 %collective-permute-start.7 = (bf16[2,256,256]{2,1,0:T(8,128)(2,1)S(1)}, bf16[2,256,256]{2,1,0:T(8,128)(2,1)S(1)}, u32[]{:S(2)}, u32[]{:S(2)}) collective-permute-start(bf16[2,256,256]{2,1,0:T(8,128)(2,1)S(1)} %copy-done.15), channel_id=1, source_target_pairs={{0,1},{1,0},{2,3},{3,2},{4,5},{5,4},{6,7},{7,6},{8,9},{9,8},{10,11... | collective-permute-start | bytes 786440 | tf_op jit(solution)/shard_map/ppermute | solution.py:478
  35.8 2.1 %collective-permute-start.8 = (bf16[2,256,256]{2,1,0:T(8,128)(2,1)S(1)}, bf16[2,256,256]{2,1,0:T(8,128)(2,1)S(1)}, u32[]{:S(2)}, u32[]{:S(2)}) collective-permute-start(bf16[2,256,256]{2,1,0:T(8,128)(2,1)S(1)} %copy-done.14), channel_id=1, source_target_pairs={{0,1},{1,0},{2,3},{3,2},{4,5},{5,4},{6,7},{7,6},{8,9},{9,8},{10,11... | collective-permute-start | bytes 786440 | tf_op jit(solution)/shard_map/ppermute | solution.py:479
  39.8 30.3 %collective-permute-start.10 = (bf16[4,256,256]{2,1,0:T(8,128)(2,1)}, bf16[4,256,256]{2,1,0:T(8,128)(2,1)S(1)}, u32[]{:S(2)}, u32[]{:S(2)}) collective-permute-start(bf16[4,256,256]{2,1,0:T(8,128)(2,1)} %get-tuple-element.37), channel_id=1, source_target_pairs={{2,0},{4,2},{6,4},{8,6},{10,8},{12,10},{14,12},{0,14},{3,1},{5,3},... | collective-permute-start | bytes 1572872 | tf_op jit(solution)/shard_map/ppermute | solution.py:504
  45.1 24.9 %collective-permute-start.9 = (bf16[4,256,256]{2,1,0:T(8,128)(2,1)}, bf16[4,256,256]{2,1,0:T(8,128)(2,1)}, u32[]{:S(2)}, u32[]{:S(2)}) collective-permute-start(bf16[4,256,256]{2,1,0:T(8,128)(2,1)} %get-tuple-element.36), channel_id=1, source_target_pairs={{0,2},{2,4},{4,6},{6,8},{8,10},{10,12},{12,14},{14,0},{1,3},{3,5},... | collective-permute-start | bytes 1572872 | tf_op jit(solution)/shard_map/ppermute | solution.py:505
  45.2 15.5 %copy-start.10 = (s32[4,64,2]{1,2,0:T(2,128)S(1)}, s32[4,64,2]{1,2,0:T(2,128)}, u32[]{:S(2)}) copy-start(s32[4,64,2]{1,2,0:T(2,128)} %param.20) | copy-start | bytes 6148
  45.2 15.5 %copy-start.13 = (s32[4,64]{1,0:T(4,128)S(1)}, s32[4,64]{1,0:T(4,128)}, u32[]{:S(2)}) copy-start(s32[4,64]{1,0:T(4,128)} %mask.1) | copy-start | bytes 3076
  58.2 5.5 %copy-start.8 = (s32[4,4]{1,0:T(4,128)S(1)}, s32[4,4]{1,0:T(4,128)}, u32[]{:S(2)}) copy-start(s32[4,4]{1,0:T(4,128)} %parent.3) | copy-start | bytes 196
  58.2 5.5 %copy-start.3 = (f32[17,256,256]{2,1,0:T(8,128)S(1)}, f32[17,256,256]{2,1,0:T(8,128)}, u32[]{:S(2)}) copy-start(f32[17,256,256]{2,1,0:T(8,128)} %near.1.near_total) | copy-start | bytes 13369348
  58.3 5.4 %collective-permute-start.5 = (bf16[512,256]{1,0:T(8,128)(2,1)S(1)}, bf16[512,256]{1,0:T(8,128)(2,1)S(1)}, u32[]{:S(2)}, u32[]{:S(2)}) collective-permute-start(bf16[512,256]{1,0:T(8,128)(2,1)S(1)} %get-tuple-element.40), channel_id=1, source_target_pairs={{0,1},{1,0},{2,3},{3,2},{4,5},{5,4},{6,7},{7,6},{8,9},{9,8},{10,11... | collective-permute-start | bytes 786440 | tf_op jit(solution)/shard_map/ppermute | solution.py:558
  58.4 5.3 %collective-permute-start.6 = (bf16[512,256]{1,0:T(8,128)(2,1)S(1)}, bf16[512,256]{1,0:T(8,128)(2,1)S(1)}, u32[]{:S(2)}, u32[]{:S(2)}) collective-permute-start(bf16[512,256]{1,0:T(8,128)(2,1)S(1)} %get-tuple-element.39), channel_id=1, source_target_pairs={{0,1},{1,0},{2,3},{3,2},{4,5},{5,4},{6,7},{7,6},{8,9},{9,8},{10,11... | collective-permute-start | bytes 786440 | tf_op jit(solution)/shard_map/ppermute | solution.py:559
where the time goes:
time: 72.8 us; the launch traced here: 72.3 us
  Pallas kernels  40.4 us (55%)
  starting transfers between devices  18.7 us (26%)
  local copies, waits for them, and re-layouts  9.12 us (13%)
  waiting for transfers between devices  2.55 us (4%)
  between operations  1.22 us (2%)
    pallas_call x9, Pallas kernels, call(): pl.pallas_call(kernel, out_shape=outs, in_specs=in_specs, out_specs=out_s...  40.4 us
    unnamed x34, local copies, waits for them, and re-layouts  7.01 us
    ppermute x1, starting transfers between devices, per_device(): from_right = lax.ppermute(first, 'gx', left)  6.06 us
    all_to_all x1, starting transfers between devices, per_device(): lax.all_to_all(jnp.broadcast_to(coeff[None], (gx_count,) + coeff.shape),...  6 us
    ppermute x1, starting transfers between devices, per_device(): to_last = lax.ppermute(back_left, 'gx', left)  5.38 us
    ppermute x1, waiting for transfers between devices, per_device(): low_corner = lax.ppermute(low_corner, 'gy', swap)  1.68 us
  transfers between devices with their start and end apart: 12, of which 3 were waited for; matrix products, arithmetic and copies ran while one was open for 7% of the time, Pallas kernels for 51%

commit v1 on v0

--- a/solution.py
+++ b/solution.py
@@ -12,7 +12,7 @@
 GROUP = 4
 DEPTH = 3
 MIB = 1024 * 1024
-VMEM_MIB = {"edges": 8, "leaf": 16, "outward": 54, "fold": 4, "itself": 16, "turn": 12, "near": 46, "far": 26, "last": 8}
+VMEM_MIB = {"edges": 8, "leaf": 16, "outward": 54, "fold": 4, "turn": 12, "near": 42, "far": 26, "last": 8}
 
 
 def dot_nn(a, b):
@@ -118,9 +118,10 @@
 
 
 def out_kernel(
-    tile_x, tile_y, half, pairs, count, bloch, own, near, left, right, low_corner, high_corner, beside, lists, win, acc, ring,
-    sems
+    tile_x, tile_y, half, pairs, count, bloch, own, near, unused, left, right, low_corner, high_corner, beside, lists, win, acc,
+    ring, sems
 ):
+    del unused
     blocks = tile_x * tile_y
     wide_x, wide_y = tile_x + 2, tile_y + 2
     panels = own.shape[2]
@@ -233,45 +234,39 @@
         coeff[q * rank : (q + 1) * rank, half:] = acc[q, rank:].astype(BF16)
 
 
-def self_kernel(blocks, half, own, own_mats, total, win, ring, sems):
-    groups = blocks // GROUP
-
-    def fetch(t, to, sem):
-        pltpu.make_async_copy(own_mats.at[t], to, sem).start()
-
-    def body(g, at):
-        for k in range(GROUP):
-            t = g * GROUP + k
-            set_pair(win, k, own[t, :half], own[t, half:], half)
-        for k in range(GROUP):
-            total[g * GROUP + k] = forward(win[k], ring[at, k])
-
-    prime, run = stream(groups, fetch, ring, sems, body)
-    prime()
-    run(0, groups)
-
-
 def near_kernel(
-    tile_x, tile_y, half, pairs, lists, bloch, own, beside, from_left, from_right, corner, begun, near, total, win, ring, sems,
-    begun_sem
+    tile_x, tile_y, half, pairs, lists, bloch, own, beside, from_left, from_right, corner, own_mats, near, total, win, ring, sems
 ):
     blocks = tile_x * tile_y
     wide_x, wide_y = tile_x + 2, tile_y + 2
     panels = own.shape[2]
     n, n_over = lists[2, 0], lists[2, 1]
-    begin = pltpu.make_async_copy(begun, total.at[pl.ds(0, blocks)], begun_sem)
-    begin.start()
     groups = groups_of(n)
+    own_groups = blocks // GROUP
     side_at, over_at = blocks, blocks + 2 * tile_x
 
     def slot(t):
         return jnp.where(t < groups * GROUP, lists[0, t], lists[1, jnp.maximum(t - groups * GROUP, 0)])
 
     def fetch(t, to, sem):
-        pltpu.make_async_copy(near.at[slot(t)], to, sem).start()
-
-    def body(g, at):
-        @pl.when(g < groups)
+        @pl.when(t < blocks)
+        def _():
+            pltpu.make_async_copy(own_mats.at[jnp.minimum(t, blocks - 1)], to, sem).start()
+
+        @pl.when(t >= blocks)
+        def _():
+            pltpu.make_async_copy(near.at[slot(jnp.maximum(t - blocks, 0))], to, sem).start()
+
+    def body(step, at):
+        g = step - own_groups
+
+        @pl.when(g < 0)
+        def _():
+            for k in range(GROUP):
+                t = step * GROUP + k
+                total[t] = forward(win[t], ring[at, k])
+
+        @pl.when((g >= 0) & (g < groups))
         def _():
             for k in range(GROUP):
                 t = g * GROUP + k
@@ -292,7 +287,7 @@
                 c = jnp.where((cx == 0) | (cx == wide_x - 1), over, side_at + jnp.where(cy == 0, 0, tile_x) + cx - 1)
                 total[jnp.where(live, r, blocks)] += forward(win[jnp.where(live, c, 0)], ring[at, k])
 
-    every_group = groups + groups_of(n_over)
+    every_group = own_groups + groups + groups_of(n_over)
     prime, run = stream(every_group, fetch, ring, sems, body)
     prime()
     for b in range(blocks):
@@ -312,7 +307,6 @@
             cos, sin = cell_phase(bloch, (wide_x - 1) * side, cy, wide_x, wide_y, panels)
             re, im = turned(cell, cos, sin, half)
             set_pair(win, over_at + side * wide_y + cy, re.astype(BF16), im.astype(BF16), half)
-    begin.wait()
     run(0, every_group)
 
 
@@ -452,10 +446,21 @@
         [jnp.concatenate([tr[:, 0], -tr[:, 1]], axis=2), jnp.concatenate([tr[:, 1], tr[:, 0]], axis=2)], axis=1
     )
 
+    coeff = call(
+        functools.partial(leaf_kernel, blocks, rank, half),
+        (parent, own, basis_b, moves, first),
+        [SMEM, VMEM, VMEM, VMEM, ANY],
+        shape(clusters * rank, width),
+        VMEM,
+        [pltpu.VMEM((clusters, 2 * rank, half), F32)],
+        2 * blocks * 2 * rank * panels * width,
+        own.size * 2 + basis_b.size * 2,
+        "leaf",
+    )
     back_left, back_right, low_corner, high_corner, beside_out, lists = call(
         functools.partial(out_kernel, tile_x, tile_y, half),
-        (pairs, near_count, bloch, own, near),
-        [SMEM, SMEM, SMEM, VMEM, ANY],
+        (pairs, near_count, bloch, own, near, coeff),
+        [SMEM, SMEM, SMEM, VMEM, ANY, ANY],
         [
             shape(tile_y, width, panels),
             shape(tile_y, width, panels),
@@ -478,17 +483,6 @@
     low_corner = lax.ppermute(low_corner, "gy", swap)
     high_corner = lax.ppermute(high_corner, "gy", swap)
     back = lax.ppermute(beside_out, "gy", swap)
-    coeff = call(
-        functools.partial(leaf_kernel, blocks, rank, half),
-        (parent, own, basis_b, moves, first),
-        [SMEM, VMEM, VMEM, VMEM, ANY],
-        shape(clusters * rank, width),
-        VMEM,
-        [pltpu.VMEM((clusters, 2 * rank, half), F32)],
-        2 * blocks * 2 * rank * panels * width,
-        own.size * 2 + basis_b.size * 2,
-        "leaf",
-    )
     back_left, back_right = call(
         functools.partial(fold_kernel, tile_y),
         (low_corner, high_corner, back_left, back_right),
@@ -504,21 +498,6 @@
     to_last = lax.ppermute(back_left, "gx", left)
     to_first = lax.ppermute(back_right, "gx", right)
 
-    self_total = call(
-        functools.partial(self_kernel, blocks, half),
-        (own, own_mats),
-        [VMEM, ANY],
-        shape(blocks, width, panels, dtype=F32),
-        VMEM,
-        [
-            pltpu.VMEM((GROUP, width, 2 * panels), BF16),
-            pltpu.VMEM((DEPTH, GROUP, 2, panels, panels), BF16),
-            pltpu.SemaphoreType.DMA((DEPTH, GROUP)),
-        ],
-        0,
-        0,
-        "itself",
-    )
     coeff = lax.all_to_all(jnp.broadcast_to(coeff[None], (gx_count,) + coeff.shape), "gx", 0, 0).reshape(-1, width)
     mats = coupling.transpose(0, 2, 1, 3)
     sources = 2 * mats.shape[2]
@@ -534,12 +513,12 @@
         "turn",
     )
 
-    from_left, from_right, _ = lax.optimization_barrier((from_left, from_right, self_total))
+    from_left, from_right, _ = lax.optimization_barrier((from_left, from_right, back_left))
     halo_corner = jnp.stack([from_left[0], from_left[tile_y - 1], from_right[0], from_right[tile_y - 1]])
     halo_corner = lax.ppermute(halo_corner, "gy", swap)
     near_total = call(
         functools.partial(near_kernel, tile_x, tile_y, half),
-        (pairs, lists, bloch, own, beside, from_left, from_right, halo_corner, self_total, near),
+        (pairs, lists, bloch, own, beside, from_left, from_right, halo_corner, own_mats, near),
         [SMEM] * 3 + [VMEM] * 5 + [ANY, ANY],
         shape(blocks + 1, width, panels, dtype=F32),
         VMEM,
@@ -547,7 +526,6 @@
             pltpu.VMEM((blocks + 2 * tile_x + 2 * wide_y, width, 2 * panels), BF16),
             pltpu.VMEM((DEPTH, GROUP, 2, panels, panels), BF16),
             pltpu.SemaphoreType.DMA((DEPTH, GROUP)),
-            pltpu.SemaphoreType.DMA,
         ],
         0,
         0,

time: 72.8 us -> 71.7 us (0.985)
  starting transfers between devices: 18.7 us -> 17.7 us
    ppermute x1, starting transfers between devices: 0.01 us -> 3.02 us  [per_device(): from_left = lax.ppermute(last, 'gx', right)]
    ppermute x1, starting transfers between devices: 6.06 us -> 3.1 us  [per_device(): from_right = lax.ppermute(first, 'gx', left)]
    all_to_all x1, starting transfers between devices: 6 us -> 3.49 us  [per_device(): lax.all_to_all(jnp.broadcast_to(coeff[None], (gx_count,) + coeff.shape),...]
    ppermute x1, waiting for transfers between devices: 1.68 us -> 0.01 us  [per_device(): low_corner = lax.ppermute(low_corner, 'gy', swap)]
    ppermute x1, waiting for transfers between devices: 0.47 us -> 1.87 us  [per_device(): from_right = lax.ppermute(first, 'gx', left)]
    pallas_call x9 -> x8, Pallas kernels: 40.4 us -> 40.8 us  [call(): pl.pallas_call(kernel, out_shape=outs, in_specs=in_specs, out_specs=out_s...]
    unnamed x34 -> x30, local copies, waits for them, and re-layouts: 7.01 us -> 7.11 us
  transfers between devices with their start and end apart: 12 -> 12, of which waited for: 3 -> 1; matrix products, arithmetic and copies ran while one was open for 7% -> 7% of each run, Pallas kernels for 51% -> 52%
where the time goes in v1:
time: 71.7 us; the launch traced here: 71.1 us
  Pallas kernels  40.8 us (57%)
  starting transfers between devices  17.7 us (25%)
  local copies, waits for them, and re-layouts  9.24 us (13%)
  waiting for transfers between devices  1.9 us (3%)
  between operations  1.18 us (2%)
    pallas_call x8, Pallas kernels, call(): pl.pallas_call(kernel, out_shape=outs, in_specs=in_specs, out_specs=out_s...  40.8 us
    unnamed x30, local copies, waits for them, and re-layouts  7.11 us
    ppermute x1, starting transfers between devices, per_device(): to_last = lax.ppermute(back_left, 'gx', left)  6.09 us
    all_to_all x1, starting transfers between devices, per_device(): lax.all_to_all(jnp.broadcast_to(coeff[None], (gx_count,) + coeff.shape),...  3.49 us
    ppermute x1, starting transfers between devices, per_device(): from_right = lax.ppermute(first, 'gx', left)  3.1 us
    ppermute x1, starting transfers between devices, per_device(): from_left = lax.ppermute(last, 'gx', right)  3.02 us
    ppermute x1, waiting for transfers between devices, per_device(): from_right = lax.ppermute(first, 'gx', left)  1.87 us
  transfers between devices with their start and end apart: 12, of which 1 were waited for; matrix products, arithmetic and copies ran while one was open for 7% of the time, Pallas kernels for 52%

profile of v1, /device:TPU:0, one launch (start us, length us, event | category | flops | bytes accessed | tf_op | source)
XLA Modules:
  0.0 71.1 jit_solution(2730607564769473381)
XLA Ops:
  0.0 1.6 %copy-done = bf16[4,4,2,128,256]{4,3,2,1,0:T(8,128)(2,1)S(1)} copy-done((bf16[4,4,2,128,256]{4,3,2,1,0:T(8,128)(2,1)S(1)}, bf16[4,4,2,128,256]{4,3,2,1,0:T(8,128)(2,1)}, u32[]{:S(2)}) %copy-start) | copy-done | bytes 2097176
  1.6 1.4 %edges.1 = (bf16[4,256,256]{2,1,0:T(8,128)(2,1)}, bf16[4,256,256]{2,1,0:T(8,128)(2,1)}, bf16[2,4,256,256]{3,2,1,0:T(8,128)(2,1)}) custom-call(bf16[16,256,256]{2,1,0:T(8,128)(2,1)S(1)} %bitcast.22), custom_call_target="tpu_custom_call" | custom-call | tf_op jit(solution)/shard_map/edges/pallas_call | solution.py:390
  3.0 3.0 %collective-permute-start.2 = (bf16[4,256,256]{2,1,0:T(8,128)(2,1)}, bf16[4,256,256]{2,1,0:T(8,128)(2,1)S(1)}, u32[]{:S(2)}, u32[]{:S(2)}) collective-permute-start(bf16[4,256,256]{2,1,0:T(8,128)(2,1)} %get-tuple-element.26), channel_id=1, source_target_pairs={{0,2},{2,4},{4,6},{6,8},{8,10},{10,12},{12,14},{14,0},{1,3},{3,5},... | collective-permute-start | bytes 1572872 | tf_op jit(solution)/shard_map/ppermute | solution.py:437
  6.0 3.1 %collective-permute-start.3 = (bf16[4,256,256]{2,1,0:T(8,128)(2,1)}, bf16[4,256,256]{2,1,0:T(8,128)(2,1)}, u32[]{:S(2)}, u32[]{:S(2)}) collective-permute-start(bf16[4,256,256]{2,1,0:T(8,128)(2,1)} %get-tuple-element.22.unused), channel_id=1, source_target_pairs={{2,0},{4,2},{6,4},{8,6},{10,8},{12,10},{14,12},{0,14},{3,1},{5,3},... | collective-permute-start | bytes 1572872 | tf_op jit(solution)/shard_map/ppermute | solution.py:438
  9.8 0.9 %copy.16 = bf16[4,4,2,1024]{3,1,0,2:T(4,128)(2,1)S(1)} copy(bf16[4,4,2,1024]{3,2,1,0:T(2,128)(2,1)} %param.18) | data formatting | bytes 131072 | tf_op args[6]
  10.6 0.2 reshape.29
  10.9 0.2 maximum_maximum_fusion.moves
  11.1 3.2 %leaf.1.unused = bf16[128,256]{1,0:T(8,128)(2,1)S(1)} custom-call(s32[4,4]{1,0:T(4,128)S(1)} %copy-done.8, bf16[16,256,256]{2,1,0:T(8,128)(2,1)S(1)} %bitcast.23, bf16[16,64,256]{2,1,0:T(8,128)(2,1)S(1)} %bitcast.29, bf16[16,64,64]{2,1,0:T(8,128)(2,1)S(1)} %maximum_maximum_fusion.moves, bf16[4,256,256]{2,1,0:T(8,128)(2,1)} %get-tuple-element.22.unused), custom_call_target="tpu_custom_call" | custom-call | flops 1342177 | bytes 26214 | tf_op jit(solution)/shard_map/leaf/pallas_call | solution.py:390
  14.3 0.6 copy-done.6
  14.9 7.2 %outward.1 = (bf16[4,256,256]{2,1,0:T(8,128)(2,1)}, bf16[4,256,256]{2,1,0:T(8,128)(2,1)}, bf16[2,256,256]{2,1,0:T(8,128)(2,1)}, bf16[2,256,256]{2,1,0:T(8,128)(2...) custom-call(s32[2,40]{1,0:T(2,128)} %bitcast.32, s32[1,1]{1,0:T(1,128)S(6)} %copy.23.count, f32[2]{0:T(128)} %bloch.5, ...), custom_call_target="tpu_custom_call" | custom-call | flops 6710886 | bytes 47185 | tf_op jit(solution)/shard_map/outward/pallas_call | solution.py:390
  22.1 0.1 collective-permute-start.4
  22.2 0.5 collective-permute-start.5
  22.7 0.1 collective-permute-start.1
  22.8 0.8 %broadcast_in_dim.2 = bf16[8,128,256]{2,1,0:T(8,128)(2,1)} broadcast(bf16[128,256]{1,0:T(8,128)(2,1)S(1)} %copy-done.7), dimensions={1,2} | broadcast | bytes 589824 | tf_op jit(solution)/shard_map/broadcast_in_dim | solution.py:501
  23.6 3.5 %all-to-all-start = ((bf16[8,128,256]{2,1,0:T(8,128)(2,1)}), bf16[8,128,256]{2,1,0:T(8,128)(2,1)S(1)}, u32[]{:S(2)}, u32[]{:S(2)}) async-start(bf16[8,128,256]{2,1,0:T(8,128)(2,1)} %broadcast_in_dim.2), calls=%async_computation | async-start | bytes 1048576 | tf_op jit(solution)/shard_map/all_to_all | solution.py:501
  27.1 0.0 copy-start.2
  27.1 0.5 collective-permute-start
  27.6 2.0 %fold.1 = (bf16[4,256,256]{2,1,0:T(8,128)(2,1)}, bf16[4,256,256]{2,1,0:T(8,128)(2,1)}) custom-call(bf16[2,256,256]{2,1,0:T(8,128)(2,1)S(1)} %collective-permute-done.4.low_corner, bf16[2,256,256]{2,1,0:T(8,128)(2,1)S(1)} %collective-permute-done.5.high_corner, ...), custom_call_target="tpu_custom_call", output_to_operand_aliasing={{0}: (2, {}), {1}: (3, {})} | custom-call | tf_op jit(solution)/shard_map/fold/pallas_call | solution.py:390
  29.6 1.9 %collective-permute-done.3.from_right = bf16[4,256,256]{2,1,0:T(8,128)(2,1)} collective-permute-done((bf16[4,256,256]{2,1,0:T(8,128)(2,1)}, bf16[4,256,256]{2,1,0:T(8,128)(2,1)}, u32[]{:S(2)}, u32[]{:S(2)}) %collective-permute-start.3) | collective-permute-done | bytes 524320 | tf_op jit(solution)/shard_map/ppermute | solution.py:438
  31.5 1.0 %fusion.2 = (bf16[1,256,256]{2,1,0:T(8,128)(2,1)S(1)}, bf16[1,256,256]{2,1,0:T(8,128)(2,1)S(1)}, bf16[1,256,256]{2,1,0:T(8,128)(2,1)S(1)}, bf16[1,256,256]{2,1,0:T(8,128)(2,1)S(1)}) fusion(bf16[4,256,256]{2,1,0:T(8,128)(2,1)S(1)} %collective-permute-done.2.from_left, bf16[4,256,256]{2,1,0:T(8,128)(2,1)} %collective-permute-done.3.from_right), kind=kLoop, calls=%fused_computation.7 | loop fusion | bytes 1048576 | tf_op jit(solution)/shard_map/slice | solution.py:517
  32.5 0.1 pad_maximum_fusion
  32.6 0.1 collective-permute-start.6
  32.7 0.2 collective-permute-start.9
  32.9 6.1 %collective-permute-start.10 = (bf16[4,256,256]{2,1,0:T(8,128)(2,1)}, bf16[4,256,256]{2,1,0:T(8,128)(2,1)}, u32[]{:S(2)}, u32[]{:S(2)}) collective-permute-start(bf16[4,256,256]{2,1,0:T(8,128)(2,1)} %get-tuple-element.31), channel_id=1, source_target_pairs={{2,0},{4,2},{6,4},{8,6},{10,8},{12,10},{14,12},{0,14},{3,1},{5,3},... | collective-permute-start | bytes 1572872 | tf_op jit(solution)/shard_map/ppermute | solution.py:498
  39.1 2.2 %copy-done.4 = bf16[4,4,2,256,256]{4,3,2,1,0:T(8,128)(2,1)S(1)} copy-done((bf16[4,4,2,256,256]{4,3,2,1,0:T(8,128)(2,1)S(1)}, bf16[4,4,2,256,256]{4,3,2,1,0:T(8,128)(2,1)}, u32[]{:S(2)}) %copy-start.4) | copy-done | bytes 4194328
  41.2 15.7 %near.1.near_total = f32[17,256,256]{2,1,0:T(8,128)} custom-call(s32[2,40]{1,0:T(2,128)S(1)} %bitcast.33, s32[3,48]{1,0:T(4,128)S(1)} %copy-done.12, f32[2]{0:T(128)S(1)} %copy-done.9, bf16[16,256,256]{2,1,0:T(8,128)(2,1)S(1)} %bitcast.24, bf16[2,4,256,256]{3,2,1,0:T(8,128)(2,1)} %collective-permute-done.1.beside, ...), custom_call_target="tpu_custom_call" | custom-call | tf_op jit(solution)/shard_map/near/pallas_call | solution.py:390
  57.0 0.1 collective-permute-start.8
  57.1 0.5 collective-permute-start.7
  57.6 1.8 %copy.19 = bf16[4,64,2,1024]{3,1,2,0:T(8,128)(2,1)S(1)} copy(bf16[4,64,2,1024]{3,2,1,0:T(2,128)(2,1)} %param.19) | data formatting | bytes 2097152 | tf_op args[7]
  59.4 3.0 %turn.1.coupling = bf16[32,128,128]{2,1,0:T(8,128)(2,1)S(1)} custom-call(f32[2]{0:T(128)S(1)} %copy-done.9, s32[4,2,64]{2,1,0:T(2,128)S(1)} %bitcast.31, s32[4,64]{1,0:T(4,128)S(1)} %copy-done.13, bf16[4,2,64,1024]{3,2,1,0:T(8,128)(2,1)S(1)} %bitcast.27), custom_call_target="tpu_custom_call" | custom-call | tf_op jit(solution)/shard_map/turn/pallas_call | solution.py:390
  62.5 6.3 %far.1 = (bf16[16,256,256]{2,1,0:T(8,128)(2,1)}, f32[8,256,256]{2,1,0:T(8,128)S(1)}) custom-call(s32[4,4]{1,0:T(4,128)S(1)} %copy-done.8, bf16[2,4,256,256]{3,2,1,0:T(8,128)(2,1)S(1)} %collective-permute-done.back, bf16[1024,256]{1,0:T(8,128)(2,1)S(1)} %bitcast.26, bf16[512,256]{1,0:T(8,128)(2,1)S(1)} %collective-permute-done.7.other_low, ...), custom_call_target="tpu_custom_call" | custom-call | tf_op jit(solution)/shard_map/far/pallas_call | solution.py:390
  68.8 2.1 %last.1 = bf16[16,256,256]{2,1,0:T(8,128)(2,1)} custom-call(f32[8,256,256]{2,1,0:T(8,128)S(1)} %get-tuple-element.36.edge, bf16[4,256,256]{2,1,0:T(8,128)(2,1)S(1)} %collective-permute-done.9.to_first, bf16[4,256,256]{2,1,0:T(8,128)(2,1)} %collective-permute-done.10.to_last, ...), custom_call_target="tpu_custom_call", output_to_operand_aliasing={{}: (3, {})} | custom-call | tf_op jit(solution)/shard_map/last/pallas_call | solution.py:390
  (38 shorter events, 0.2 us)
Async XLA Ops:
  0.0 1.6 %copy-start = (bf16[4,4,2,128,256]{4,3,2,1,0:T(8,128)(2,1)S(1)}, bf16[4,4,2,128,256]{4,3,2,1,0:T(8,128)(2,1)}, u32[]{:S(2)}) copy-start(bf16[4,4,2,128,256]{4,3,2,1,0:T(8,128)(2,1)} %param.12) | copy-start | bytes 6291460
  1.6 9.5 %copy-start.1 = (bf16[4,4,2,128,256]{4,3,2,1,0:T(8,128)(2,1)S(1)}, bf16[4,4,2,128,256]{4,3,2,1,0:T(8,128)(2,1)}, u32[]{:S(2)}) copy-start(bf16[4,4,2,128,256]{4,3,2,1,0:T(8,128)(2,1)} %param.12) | copy-start | bytes 6291460
  1.6 9.5 %copy-start.5 = (bf16[4,4,2,32,256]{4,3,2,1,0:T(8,128)(2,1)S(1)}, bf16[4,4,2,32,256]{4,3,2,1,0:T(8,128)(2,1)}, u32[]{:S(2)}) copy-start(bf16[4,4,2,32,256]{4,3,2,1,0:T(8,128)(2,1)} %param.17) | copy-start | bytes 1572868
  1.6 9.5 %copy-start.8 = (s32[4,4]{1,0:T(4,128)S(1)}, s32[4,4]{1,0:T(4,128)}, u32[]{:S(2)}) copy-start(s32[4,4]{1,0:T(4,128)} %parent.3) | copy-start | bytes 196
  3.0 26.6 %collective-permute-start.2 = (bf16[4,256,256]{2,1,0:T(8,128)(2,1)}, bf16[4,256,256]{2,1,0:T(8,128)(2,1)S(1)}, u32[]{:S(2)}, u32[]{:S(2)}) collective-permute-start(bf16[4,256,256]{2,1,0:T(8,128)(2,1)} %get-tuple-element.26), channel_id=1, source_target_pairs={{0,2},{2,4},{4,6},{6,8},{8,10},{10,12},{12,14},{14,0},{1,3},{3,5},... | collective-permute-start | bytes 1572872 | tf_op jit(solution)/shard_map/ppermute | solution.py:437
  6.0 25.5 %collective-permute-start.3 = (bf16[4,256,256]{2,1,0:T(8,128)(2,1)}, bf16[4,256,256]{2,1,0:T(8,128)(2,1)}, u32[]{:S(2)}, u32[]{:S(2)}) collective-permute-start(bf16[4,256,256]{2,1,0:T(8,128)(2,1)} %get-tuple-element.22.unused), channel_id=1, source_target_pairs={{2,0},{4,2},{6,4},{8,6},{10,8},{12,10},{14,12},{0,14},{3,1},{5,3},... | collective-permute-start | bytes 1572872 | tf_op jit(solution)/shard_map/ppermute | solution.py:438
  14.3 0.6 copy-start.6
  14.9 7.9 %copy-start.7 = (bf16[128,256]{1,0:T(8,128)(2,1)S(1)}, bf16[128,256]{1,0:T(8,128)(2,1)}, u32[]{:S(2)}) copy-start(bf16[128,256]{1,0:T(8,128)(2,1)} %copy-done.6) | copy-start | bytes 196612
  22.1 5.0 %collective-permute-start.4 = (bf16[2,256,256]{2,1,0:T(8,128)(2,1)}, bf16[2,256,256]{2,1,0:T(8,128)(2,1)S(1)}, u32[]{:S(2)}, u32[]{:S(2)}) collective-permute-start(bf16[2,256,256]{2,1,0:T(8,128)(2,1)} %get-tuple-element.27), channel_id=1, source_target_pairs={{0,1},{1,0},{2,3},{3,2},{4,5},{5,4},{6,7},{7,6},{8,9},{9,8},{10,11... | collective-permute-start | bytes 786440 | tf_op jit(solution)/shard_map/ppermute | solution.py:483
  22.2 5.5 %collective-permute-start.5 = (bf16[2,256,256]{2,1,0:T(8,128)(2,1)}, bf16[2,256,256]{2,1,0:T(8,128)(2,1)S(1)}, u32[]{:S(2)}, u32[]{:S(2)}) collective-permute-start(bf16[2,256,256]{2,1,0:T(8,128)(2,1)} %get-tuple-element.28), channel_id=1, source_target_pairs={{0,1},{1,0},{2,3},{3,2},{4,5},{5,4},{6,7},{7,6},{8,9},{9,8},{10,11... | collective-permute-start | bytes 786440 | tf_op jit(solution)/shard_map/ppermute | solution.py:484
  22.7 16.3 %collective-permute-start.1 = (bf16[2,4,256,256]{3,2,1,0:T(8,128)(2,1)}, bf16[2,4,256,256]{3,2,1,0:T(8,128)(2,1)}, u32[]{:S(2)}, u32[]{:S(2)}) collective-permute-start(bf16[2,4,256,256]{3,2,1,0:T(8,128)(2,1)} %get-tuple-element.25), channel_id=1, source_target_pairs={{0,1},{1,0},{2,3},{3,2},{4,5},{5,4},{6,7},{7,6},{8,9},{9,8},{10,11... | collective-permute-start | bytes 3145736 | tf_op jit(solution)/shard_map/ppermute | solution.py:439
  23.6 33.4 %all-to-all-start = ((bf16[8,128,256]{2,1,0:T(8,128)(2,1)}), bf16[8,128,256]{2,1,0:T(8,128)(2,1)S(1)}, u32[]{:S(2)}, u32[]{:S(2)}) async-start(bf16[8,128,256]{2,1,0:T(8,128)(2,1)} %broadcast_in_dim.2), calls=%async_computation | async-start | bytes 1048576 | tf_op jit(solution)/shard_map/all_to_all | solution.py:501
  27.1 11.9 %copy-start.2 = (bf16[4,4,2,128,256]{4,3,2,1,0:T(8,128)(2,1)S(1)}, bf16[4,4,2,128,256]{4,3,2,1,0:T(8,128)(2,1)}, u32[]{:S(2)}) copy-start(bf16[4,4,2,128,256]{4,3,2,1,0:T(8,128)(2,1)} %param.12) | copy-start | bytes 6291460
  27.1 11.9 %copy-start.9 = (f32[2]{0:T(128)S(1)}, f32[2]{0:T(128)}, u32[]{:S(2)}) copy-start(f32[2]{0:T(128)} %bloch.5) | copy-start | bytes 28
  27.1 11.9 %copy-start.11 = (s32[1,1,40,2]{2,3,1,0:T(2,128)S(1)}, s32[1,1,40,2]{2,3,1,0:T(2,128)}, u32[]{:S(2)}) copy-start(s32[1,1,40,2]{2,3,1,0:T(2,128)} %param.15) | copy-start | bytes 964
  27.1 11.9 %copy-start.12 = (s32[3,48]{1,0:T(4,128)S(1)}, s32[3,48]{1,0:T(4,128)}, u32[]{:S(2)}) copy-start(s32[3,48]{1,0:T(4,128)} %get-tuple-element.24.lists) | copy-start | bytes 1732
  27.1 35.3 %collective-permute-start = (bf16[2,4,256,256]{3,2,1,0:T(8,128)(2,1)}, bf16[2,4,256,256]{3,2,1,0:T(8,128)(2,1)S(1)}, u32[]{:S(2)}, u32[]{:S(2)}) collective-permute-start(bf16[2,4,256,256]{3,2,1,0:T(8,128)(2,1)} %get-tuple-element.23), channel_id=1, source_target_pairs={{0,1},{1,0},{2,3},{3,2},{4,5},{5,4},{6,7},{7,6},{8,9},{9,8},{10,11... | collective-permute-start | bytes 3145736 | tf_op jit(solution)/shard_map/ppermute | solution.py:485
  32.6 6.4 %collective-permute-start.6 = (bf16[4,256,256]{2,1,0:T(8,128)(2,1)S(1)}, bf16[4,256,256]{2,1,0:T(8,128)(2,1)S(1)}, u32[]{:S(2)}, u32[]{:S(2)}) collective-permute-start(bf16[4,256,256]{2,1,0:T(8,128)(2,1)S(1)} %pad_maximum_fusion), channel_id=1, source_target_pairs={{0,1},{1,0},{2,3},{3,2},{4,5},{5,4},{6,7},{7,6},{8,9},{9,8},{10,11... | collective-permute-start | bytes 1572872 | tf_op jit(solution)/shard_map/ppermute | solution.py:518
  32.7 36.1 %collective-permute-start.9 = (bf16[4,256,256]{2,1,0:T(8,128)(2,1)}, bf16[4,256,256]{2,1,0:T(8,128)(2,1)S(1)}, u32[]{:S(2)}, u32[]{:S(2)}) collective-permute-start(bf16[4,256,256]{2,1,0:T(8,128)(2,1)} %get-tuple-element.37), channel_id=1, source_target_pairs={{0,2},{2,4},{4,6},{6,8},{8,10},{10,12},{12,14},{14,0},{1,3},{3,5},... | collective-permute-start | bytes 1572872 | tf_op jit(solution)/shard_map/ppermute | solution.py:499
  32.9 35.9 %collective-permute-start.10 = (bf16[4,256,256]{2,1,0:T(8,128)(2,1)}, bf16[4,256,256]{2,1,0:T(8,128)(2,1)}, u32[]{:S(2)}, u32[]{:S(2)}) collective-permute-start(bf16[4,256,256]{2,1,0:T(8,128)(2,1)} %get-tuple-element.31), channel_id=1, source_target_pairs={{2,0},{4,2},{6,4},{8,6},{10,8},{12,10},{14,12},{0,14},{3,1},{5,3},... | collective-permute-start | bytes 1572872 | tf_op jit(solution)/shard_map/ppermute | solution.py:498
  39.0 2.2 %copy-start.4 = (bf16[4,4,2,256,256]{4,3,2,1,0:T(8,128)(2,1)S(1)}, bf16[4,4,2,256,256]{4,3,2,1,0:T(8,128)(2,1)}, u32[]{:S(2)}) copy-start(bf16[4,4,2,256,256]{4,3,2,1,0:T(8,128)(2,1)} %param.13) | copy-start | bytes 12582916
  56.9 2.5 %copy-start.10 = (s32[4,64,2]{1,2,0:T(2,128)S(1)}, s32[4,64,2]{1,2,0:T(2,128)}, u32[]{:S(2)}) copy-start(s32[4,64,2]{1,2,0:T(2,128)} %param.20) | copy-start | bytes 6148
  56.9 2.5 %copy-start.13 = (s32[4,64]{1,0:T(4,128)S(1)}, s32[4,64]{1,0:T(4,128)}, u32[]{:S(2)}) copy-start(s32[4,64]{1,0:T(4,128)} %mask.1) | copy-start | bytes 3076
  57.0 5.5 %copy-start.3 = (f32[17,256,256]{2,1,0:T(8,128)S(1)}, f32[17,256,256]{2,1,0:T(8,128)}, u32[]{:S(2)}) copy-start(f32[17,256,256]{2,1,0:T(8,128)} %near.1.near_total) | copy-start | bytes 13369348
  57.0 5.4 %collective-permute-start.8 = (bf16[512,256]{1,0:T(8,128)(2,1)S(1)}, bf16[512,256]{1,0:T(8,128)(2,1)S(1)}, u32[]{:S(2)}, u32[]{:S(2)}) collective-permute-start(bf16[512,256]{1,0:T(8,128)(2,1)S(1)} %get-tuple-element.39), channel_id=1, source_target_pairs={{0,1},{1,0},{2,3},{3,2},{4,5},{5,4},{6,7},{7,6},{8,9},{9,8},{10,11... | collective-permute-start | bytes 786440 | tf_op jit(solution)/shard_map/ppermute | solution.py:537
  57.1 5.3 %collective-permute-start.7 = (bf16[512,256]{1,0:T(8,128)(2,1)S(1)}, bf16[512,256]{1,0:T(8,128)(2,1)S(1)}, u32[]{:S(2)}, u32[]{:S(2)}) collective-permute-start(bf16[512,256]{1,0:T(8,128)(2,1)S(1)} %get-tuple-element.40), channel_id=1, source_target_pairs={{0,1},{1,0},{2,3},{3,2},{4,5},{5,4},{6,7},{7,6},{8,9},{9,8},{10,11... | collective-permute-start | bytes 786440 | tf_op jit(solution)/shard_map/ppermute | solution.py:536

commit v2 on v1

--- a/solution.py
+++ b/solution.py
@@ -12,7 +12,7 @@
 GROUP = 4
 DEPTH = 3
 MIB = 1024 * 1024
-VMEM_MIB = {"edges": 8, "leaf": 16, "outward": 54, "fold": 4, "turn": 12, "near": 42, "far": 26, "last": 8}
+VMEM_MIB = {"edges": 8, "leaf": 16, "outward": 54, "fold": 4, "turn": 12, "near": 50, "far": 26, "last": 8}
 
 
 def dot_nn(a, b):

time: 71.7 us -> 67.9 us (0.947)
  Pallas kernels: 40.8 us -> 33.1 us
  starting transfers between devices: 17.7 us -> 23.2 us
  local copies, waits for them, and re-layouts: 9.24 us -> 6.74 us
    pallas_call x8, Pallas kernels: 40.8 us -> 33.1 us  [call(): pl.pallas_call(kernel, out_shape=outs, in_specs=in_specs, out_specs=out_s...]
    ppermute x1, starting transfers between devices: 0.07 us -> 4.68 us  [per_device(): other_high = lax.ppermute(coeff[middle:], 'gy', swap)]
    unnamed x30 -> x26, local copies, waits for them, and re-layouts: 7.11 us -> 4.61 us
    ppermute x1, starting transfers between devices: 0.07 us -> 1.22 us  [per_device(): low_corner = lax.ppermute(low_corner, 'gy', swap)]
    ppermute x1, starting transfers between devices: 6.09 us -> 4.97 us  [per_device(): to_last = lax.ppermute(back_left, 'gx', left)]
    ppermute x1, starting transfers between devices: 0.23 us -> 1.2 us  [per_device(): to_first = lax.ppermute(back_right, 'gx', right)]
  transfers between devices with their start and end apart: 12 -> 12, of which waited for: 1 -> 2; matrix products, arithmetic and copies ran while one was open for 7% -> 7% of each run, Pallas kernels for 52% -> 44%
where the time goes in v2:
time: 67.9 us; the launch traced here: 66.9 us
  Pallas kernels  33.1 us (49%)
  starting transfers between devices  23.2 us (34%)
  local copies, waits for them, and re-layouts  6.74 us (10%)
  waiting for transfers between devices  2.49 us (4%)
  between operations  1.12 us (2%)
    pallas_call x8, Pallas kernels, call(): pl.pallas_call(kernel, out_shape=outs, in_specs=in_specs, out_specs=out_s...  33.1 us
    ppermute x1, starting transfers between devices, per_device(): to_last = lax.ppermute(back_left, 'gx', left)  4.97 us
    ppermute x1, starting transfers between devices, per_device(): other_high = lax.ppermute(coeff[middle:], 'gy', swap)  4.68 us
    unnamed x26, local copies, waits for them, and re-layouts  4.61 us
    all_to_all x1, starting transfers between devices, per_device(): lax.all_to_all(jnp.broadcast_to(coeff[None], (gx_count,) + coeff.shape),...  4.12 us
    ppermute x1, starting transfers between devices, per_device(): from_right = lax.ppermute(first, 'gx', left)  3.1 us
    ppermute x1, starting transfers between devices, per_device(): from_left = lax.ppermute(last, 'gx', right)  3.02 us
    ppermute x1, waiting for transfers between devices, per_device(): from_right = lax.ppermute(first, 'gx', left)  2.29 us
  transfers between devices with their start and end apart: 12, of which 2 were waited for; matrix products, arithmetic and copies ran while one was open for 7% of the time, Pallas kernels for 44%

profile of v2, /device:TPU:0, one launch (start us, length us, event | category | flops | bytes accessed | tf_op | source)
XLA Modules:
  0.0 66.9 jit_solution(6119773205132658510)
XLA Ops:
  0.0 1.6 %copy-done = bf16[4,4,2,128,256]{4,3,2,1,0:T(8,128)(2,1)S(1)} copy-done((bf16[4,4,2,128,256]{4,3,2,1,0:T(8,128)(2,1)S(1)}, bf16[4,4,2,128,256]{4,3,2,1,0:T(8,128)(2,1)}, u32[]{:S(2)}) %copy-start) | copy-done | bytes 2097176
  1.6 1.4 %edges.1 = (bf16[4,256,256]{2,1,0:T(8,128)(2,1)}, bf16[4,256,256]{2,1,0:T(8,128)(2,1)}, bf16[2,4,256,256]{3,2,1,0:T(8,128)(2,1)}) custom-call(bf16[16,256,256]{2,1,0:T(8,128)(2,1)S(1)} %bitcast.23), custom_call_target="tpu_custom_call" | custom-call | tf_op jit(solution)/shard_map/edges/pallas_call | solution.py:390
  3.0 3.0 %collective-permute-start.2 = (bf16[4,256,256]{2,1,0:T(8,128)(2,1)}, bf16[4,256,256]{2,1,0:T(8,128)(2,1)S(1)}, u32[]{:S(2)}, u32[]{:S(2)}) collective-permute-start(bf16[4,256,256]{2,1,0:T(8,128)(2,1)} %get-tuple-element.26), channel_id=1, source_target_pairs={{0,2},{2,4},{4,6},{6,8},{8,10},{10,12},{12,14},{14,0},{1,3},{3,5},... | collective-permute-start | bytes 1572872 | tf_op jit(solution)/shard_map/ppermute | solution.py:437
  6.0 3.1 %collective-permute-start.3 = (bf16[4,256,256]{2,1,0:T(8,128)(2,1)}, bf16[4,256,256]{2,1,0:T(8,128)(2,1)}, u32[]{:S(2)}, u32[]{:S(2)}) collective-permute-start(bf16[4,256,256]{2,1,0:T(8,128)(2,1)} %get-tuple-element.22.unused), channel_id=1, source_target_pairs={{2,0},{4,2},{6,4},{8,6},{10,8},{12,10},{14,12},{0,14},{3,1},{5,3},... | collective-permute-start | bytes 1572872 | tf_op jit(solution)/shard_map/ppermute | solution.py:438
  9.8 0.9 %copy.16 = bf16[4,4,2,1024]{3,1,0,2:T(4,128)(2,1)S(1)} copy(bf16[4,4,2,1024]{3,2,1,0:T(2,128)(2,1)} %param.18) | data formatting | bytes 131072 | tf_op args[6]
  10.6 0.2 reshape.29
  10.9 0.2 maximum_maximum_fusion.moves
  11.1 3.2 %leaf.1.unused = bf16[128,256]{1,0:T(8,128)(2,1)S(1)} custom-call(s32[4,4]{1,0:T(4,128)S(1)} %copy-done.6, bf16[16,256,256]{2,1,0:T(8,128)(2,1)S(1)} %bitcast.24, bf16[16,64,256]{2,1,0:T(8,128)(2,1)S(1)} %bitcast.28, bf16[16,64,64]{2,1,0:T(8,128)(2,1)S(1)} %maximum_maximum_fusion.moves, bf16[4,256,256]{2,1,0:T(8,128)(2,1)} %get-tuple-element.22.unused), custom_call_target="tpu_custom_call" | custom-call | flops 1342177 | bytes 26214 | tf_op jit(solution)/shard_map/leaf/pallas_call | solution.py:390
  14.3 0.6 copy-done.4
  14.9 5.5 %outward.1 = (bf16[4,256,256]{2,1,0:T(8,128)(2,1)}, bf16[4,256,256]{2,1,0:T(8,128)(2,1)}, bf16[2,256,256]{2,1,0:T(8,128)(2,1)}, bf16[2,256,256]{2,1,0:T(8,128)(2...) custom-call(s32[2,40]{1,0:T(2,128)} %bitcast.31, s32[1,1]{1,0:T(1,128)S(6)} %copy.23.count, f32[2]{0:T(128)} %bloch.5, ...), custom_call_target="tpu_custom_call" | custom-call | flops 6710886 | bytes 47185 | tf_op jit(solution)/shard_map/outward/pallas_call | solution.py:390
  20.4 1.2 %collective-permute-start.4 = (bf16[2,256,256]{2,1,0:T(8,128)(2,1)}, bf16[2,256,256]{2,1,0:T(8,128)(2,1)S(1)}, u32[]{:S(2)}, u32[]{:S(2)}) collective-permute-start(bf16[2,256,256]{2,1,0:T(8,128)(2,1)} %get-tuple-element.27), channel_id=1, source_target_pairs={{0,1},{1,0},{2,3},{3,2},{4,5},{5,4},{6,7},{7,6},{8,9},{9,8},{10,11... | collective-permute-start | bytes 786440 | tf_op jit(solution)/shard_map/ppermute | solution.py:483
  21.6 0.1 collective-permute-start.5
  21.7 0.4 collective-permute-start.1
  22.1 0.8 %broadcast_in_dim.2 = bf16[8,128,256]{2,1,0:T(8,128)(2,1)} broadcast(bf16[128,256]{1,0:T(8,128)(2,1)S(1)} %copy-done.5), dimensions={1,2} | broadcast | bytes 589824 | tf_op jit(solution)/shard_map/broadcast_in_dim | solution.py:501
  22.9 4.1 %all-to-all-start = ((bf16[8,128,256]{2,1,0:T(8,128)(2,1)}), bf16[8,128,256]{2,1,0:T(8,128)(2,1)S(1)}, u32[]{:S(2)}, u32[]{:S(2)}) async-start(bf16[8,128,256]{2,1,0:T(8,128)(2,1)} %broadcast_in_dim.2), calls=%async_computation | async-start | bytes 1048576 | tf_op jit(solution)/shard_map/all_to_all | solution.py:501
  27.1 0.0 copy-start.9
  27.1 0.2 collective-permute-start
  27.3 1.8 %fold.1 = (bf16[4,256,256]{2,1,0:T(8,128)(2,1)}, bf16[4,256,256]{2,1,0:T(8,128)(2,1)}) custom-call(bf16[2,256,256]{2,1,0:T(8,128)(2,1)S(1)} %collective-permute-done.4.low_corner, bf16[2,256,256]{2,1,0:T(8,128)(2,1)S(1)} %collective-permute-done.5.high_corner, ...), custom_call_target="tpu_custom_call", output_to_operand_aliasing={{0}: (2, {}), {1}: (3, {})} | custom-call | tf_op jit(solution)/shard_map/fold/pallas_call | solution.py:390
  29.2 0.2 collective-permute-done.2.from_left
  29.4 2.3 %collective-permute-done.3.from_right = bf16[4,256,256]{2,1,0:T(8,128)(2,1)} collective-permute-done((bf16[4,256,256]{2,1,0:T(8,128)(2,1)}, bf16[4,256,256]{2,1,0:T(8,128)(2,1)}, u32[]{:S(2)}, u32[]{:S(2)}) %collective-permute-start.3) | collective-permute-done | bytes 524320 | tf_op jit(solution)/shard_map/ppermute | solution.py:438
  31.6 1.0 %fusion.2 = (bf16[1,256,256]{2,1,0:T(8,128)(2,1)S(1)}, bf16[1,256,256]{2,1,0:T(8,128)(2,1)S(1)}, bf16[1,256,256]{2,1,0:T(8,128)(2,1)S(1)}, bf16[1,256,256]{2,1,0:T(8,128)(2,1)S(1)}) fusion(bf16[4,256,256]{2,1,0:T(8,128)(2,1)S(1)} %collective-permute-done.2.from_left, bf16[4,256,256]{2,1,0:T(8,128)(2,1)} %collective-permute-done.3.from_right), kind=kLoop, calls=%fused_computation.7 | loop fusion | bytes 1048576 | tf_op jit(solution)/shard_map/slice | solution.py:517
  32.7 0.1 pad_maximum_fusion
  32.8 0.1 collective-permute-start.6
  32.8 1.2 %collective-permute-start.9 = (bf16[4,256,256]{2,1,0:T(8,128)(2,1)}, bf16[4,256,256]{2,1,0:T(8,128)(2,1)S(1)}, u32[]{:S(2)}, u32[]{:S(2)}) collective-permute-start(bf16[4,256,256]{2,1,0:T(8,128)(2,1)} %get-tuple-element.37), channel_id=1, source_target_pairs={{0,2},{2,4},{4,6},{6,8},{8,10},{10,12},{12,14},{14,0},{1,3},{3,5},... | collective-permute-start | bytes 1572872 | tf_op jit(solution)/shard_map/ppermute | solution.py:499
  34.0 5.0 %collective-permute-start.10 = (bf16[4,256,256]{2,1,0:T(8,128)(2,1)}, bf16[4,256,256]{2,1,0:T(8,128)(2,1)}, u32[]{:S(2)}, u32[]{:S(2)}) collective-permute-start(bf16[4,256,256]{2,1,0:T(8,128)(2,1)} %get-tuple-element.31), channel_id=1, source_target_pairs={{2,0},{4,2},{6,4},{8,6},{10,8},{12,10},{14,12},{0,14},{3,1},{5,3},... | collective-permute-start | bytes 1572872 | tf_op jit(solution)/shard_map/ppermute | solution.py:498
  39.0 9.9 %near.1.near_total = f32[17,256,256]{2,1,0:T(8,128)} custom-call(s32[2,40]{1,0:T(2,128)S(1)} %bitcast.32, s32[3,48]{1,0:T(4,128)S(1)} %copy-done.10, f32[2]{0:T(128)S(1)} %copy-done.7, bf16[16,256,256]{2,1,0:T(8,128)(2,1)} %bitcast.22, bf16[2,4,256,256]{3,2,1,0:T(8,128)(2,1)} %collective-permute-done.1.beside, ...), custom_call_target="tpu_custom_call" | custom-call | tf_op jit(solution)/shard_map/near/pallas_call | solution.py:390
  49.0 4.7 %collective-permute-start.8 = (bf16[512,256]{1,0:T(8,128)(2,1)S(1)}, bf16[512,256]{1,0:T(8,128)(2,1)S(1)}, u32[]{:S(2)}, u32[]{:S(2)}) collective-permute-start(bf16[512,256]{1,0:T(8,128)(2,1)S(1)} %get-tuple-element.39), channel_id=1, source_target_pairs={{0,1},{1,0},{2,3},{3,2},{4,5},{5,4},{6,7},{7,6},{8,9},{9,8},{10,11... | collective-permute-start | bytes 786440 | tf_op jit(solution)/shard_map/ppermute | solution.py:537
  53.7 0.1 collective-permute-start.7
  53.8 1.5 %copy.19 = bf16[4,64,2,1024]{3,1,2,0:T(8,128)(2,1)S(1)} copy(bf16[4,64,2,1024]{3,2,1,0:T(2,128)(2,1)} %param.19) | data formatting | bytes 2097152 | tf_op args[7]
  55.3 3.0 %turn.1.coupling = bf16[32,128,128]{2,1,0:T(8,128)(2,1)S(1)} custom-call(f32[2]{0:T(128)S(1)} %copy-done.7, s32[4,2,64]{2,1,0:T(2,128)S(1)} %bitcast.30, s32[4,64]{1,0:T(4,128)S(1)} %copy-done.11, bf16[4,2,64,1024]{3,2,1,0:T(8,128)(2,1)S(1)} %bitcast.27), custom_call_target="tpu_custom_call" | custom-call | tf_op jit(solution)/shard_map/turn/pallas_call | solution.py:390
  58.3 6.3 %far.1 = (bf16[16,256,256]{2,1,0:T(8,128)(2,1)}, f32[8,256,256]{2,1,0:T(8,128)S(1)}) custom-call(s32[4,4]{1,0:T(4,128)S(1)} %copy-done.6, bf16[2,4,256,256]{3,2,1,0:T(8,128)(2,1)S(1)} %collective-permute-done.back, bf16[1024,256]{1,0:T(8,128)(2,1)S(1)} %bitcast.26, bf16[512,256]{1,0:T(8,128)(2,1)S(1)} %collective-permute-done.7.other_low, ...), custom_call_target="tpu_custom_call" | custom-call | tf_op jit(solution)/shard_map/far/pallas_call | solution.py:390
  64.7 2.1 %last.1 = bf16[16,256,256]{2,1,0:T(8,128)(2,1)} custom-call(f32[8,256,256]{2,1,0:T(8,128)S(1)} %get-tuple-element.36.edge, bf16[4,256,256]{2,1,0:T(8,128)(2,1)S(1)} %collective-permute-done.9.to_first, bf16[4,256,256]{2,1,0:T(8,128)(2,1)} %collective-permute-done.10.to_last, ...), custom_call_target="tpu_custom_call", output_to_operand_aliasing={{}: (3, {})} | custom-call | tf_op jit(solution)/shard_map/last/pallas_call | solution.py:390
  (34 shorter events, 0.1 us)
Async XLA Ops:
  0.0 1.6 %copy-start = (bf16[4,4,2,128,256]{4,3,2,1,0:T(8,128)(2,1)S(1)}, bf16[4,4,2,128,256]{4,3,2,1,0:T(8,128)(2,1)}, u32[]{:S(2)}) copy-start(bf16[4,4,2,128,256]{4,3,2,1,0:T(8,128)(2,1)} %param.12) | copy-start | bytes 6291460
  1.6 9.5 %copy-start.1 = (bf16[4,4,2,128,256]{4,3,2,1,0:T(8,128)(2,1)S(1)}, bf16[4,4,2,128,256]{4,3,2,1,0:T(8,128)(2,1)}, u32[]{:S(2)}) copy-start(bf16[4,4,2,128,256]{4,3,2,1,0:T(8,128)(2,1)} %param.12) | copy-start | bytes 6291460
  1.6 9.5 %copy-start.3 = (bf16[4,4,2,32,256]{4,3,2,1,0:T(8,128)(2,1)S(1)}, bf16[4,4,2,32,256]{4,3,2,1,0:T(8,128)(2,1)}, u32[]{:S(2)}) copy-start(bf16[4,4,2,32,256]{4,3,2,1,0:T(8,128)(2,1)} %param.17) | copy-start | bytes 1572868
  1.6 9.5 %copy-start.6 = (s32[4,4]{1,0:T(4,128)S(1)}, s32[4,4]{1,0:T(4,128)}, u32[]{:S(2)}) copy-start(s32[4,4]{1,0:T(4,128)} %parent.3) | copy-start | bytes 196
  3.0 26.4 %collective-permute-start.2 = (bf16[4,256,256]{2,1,0:T(8,128)(2,1)}, bf16[4,256,256]{2,1,0:T(8,128)(2,1)S(1)}, u32[]{:S(2)}, u32[]{:S(2)}) collective-permute-start(bf16[4,256,256]{2,1,0:T(8,128)(2,1)} %get-tuple-element.26), channel_id=1, source_target_pairs={{0,2},{2,4},{4,6},{6,8},{8,10},{10,12},{12,14},{14,0},{1,3},{3,5},... | collective-permute-start | bytes 1572872 | tf_op jit(solution)/shard_map/ppermute | solution.py:437
  6.0 25.6 %collective-permute-start.3 = (bf16[4,256,256]{2,1,0:T(8,128)(2,1)}, bf16[4,256,256]{2,1,0:T(8,128)(2,1)}, u32[]{:S(2)}, u32[]{:S(2)}) collective-permute-start(bf16[4,256,256]{2,1,0:T(8,128)(2,1)} %get-tuple-element.22.unused), channel_id=1, source_target_pairs={{2,0},{4,2},{6,4},{8,6},{10,8},{12,10},{14,12},{0,14},{3,1},{5,3},... | collective-permute-start | bytes 1572872 | tf_op jit(solution)/shard_map/ppermute | solution.py:438
  14.3 0.6 copy-start.4
  14.9 7.2 %copy-start.5 = (bf16[128,256]{1,0:T(8,128)(2,1)S(1)}, bf16[128,256]{1,0:T(8,128)(2,1)}, u32[]{:S(2)}) copy-start(bf16[128,256]{1,0:T(8,128)(2,1)} %copy-done.4) | copy-start | bytes 196612
  20.4 6.7 %collective-permute-start.4 = (bf16[2,256,256]{2,1,0:T(8,128)(2,1)}, bf16[2,256,256]{2,1,0:T(8,128)(2,1)S(1)}, u32[]{:S(2)}, u32[]{:S(2)}) collective-permute-start(bf16[2,256,256]{2,1,0:T(8,128)(2,1)} %get-tuple-element.27), channel_id=1, source_target_pairs={{0,1},{1,0},{2,3},{3,2},{4,5},{5,4},{6,7},{7,6},{8,9},{9,8},{10,11... | collective-permute-start | bytes 786440 | tf_op jit(solution)/shard_map/ppermute | solution.py:483
  21.6 5.7 %collective-permute-start.5 = (bf16[2,256,256]{2,1,0:T(8,128)(2,1)}, bf16[2,256,256]{2,1,0:T(8,128)(2,1)S(1)}, u32[]{:S(2)}, u32[]{:S(2)}) collective-permute-start(bf16[2,256,256]{2,1,0:T(8,128)(2,1)} %get-tuple-element.28), channel_id=1, source_target_pairs={{0,1},{1,0},{2,3},{3,2},{4,5},{5,4},{6,7},{7,6},{8,9},{9,8},{10,11... | collective-permute-start | bytes 786440 | tf_op jit(solution)/shard_map/ppermute | solution.py:484
  21.7 17.3 %collective-permute-start.1 = (bf16[2,4,256,256]{3,2,1,0:T(8,128)(2,1)}, bf16[2,4,256,256]{3,2,1,0:T(8,128)(2,1)}, u32[]{:S(2)}, u32[]{:S(2)}) collective-permute-start(bf16[2,4,256,256]{3,2,1,0:T(8,128)(2,1)} %get-tuple-element.25), channel_id=1, source_target_pairs={{0,1},{1,0},{2,3},{3,2},{4,5},{5,4},{6,7},{7,6},{8,9},{9,8},{10,11... | collective-permute-start | bytes 3145736 | tf_op jit(solution)/shard_map/ppermute | solution.py:439
  22.9 26.0 %all-to-all-start = ((bf16[8,128,256]{2,1,0:T(8,128)(2,1)}), bf16[8,128,256]{2,1,0:T(8,128)(2,1)S(1)}, u32[]{:S(2)}, u32[]{:S(2)}) async-start(bf16[8,128,256]{2,1,0:T(8,128)(2,1)} %broadcast_in_dim.2), calls=%async_computation | async-start | bytes 1048576 | tf_op jit(solution)/shard_map/all_to_all | solution.py:501
  27.1 12.0 %copy-start.7 = (f32[2]{0:T(128)S(1)}, f32[2]{0:T(128)}, u32[]{:S(2)}) copy-start(f32[2]{0:T(128)} %bloch.5) | copy-start | bytes 28
  27.1 12.0 %copy-start.9 = (s32[1,1,40,2]{2,3,1,0:T(2,128)S(1)}, s32[1,1,40,2]{2,3,1,0:T(2,128)}, u32[]{:S(2)}) copy-start(s32[1,1,40,2]{2,3,1,0:T(2,128)} %param.15) | copy-start | bytes 964
  27.1 12.0 %copy-start.10 = (s32[3,48]{1,0:T(4,128)S(1)}, s32[3,48]{1,0:T(4,128)}, u32[]{:S(2)}) copy-start(s32[3,48]{1,0:T(4,128)} %get-tuple-element.24.lists) | copy-start | bytes 1732
  27.1 31.2 %collective-permute-start = (bf16[2,4,256,256]{3,2,1,0:T(8,128)(2,1)}, bf16[2,4,256,256]{3,2,1,0:T(8,128)(2,1)S(1)}, u32[]{:S(2)}, u32[]{:S(2)}) collective-permute-start(bf16[2,4,256,256]{3,2,1,0:T(8,128)(2,1)} %get-tuple-element.23), channel_id=1, source_target_pairs={{0,1},{1,0},{2,3},{3,2},{4,5},{5,4},{6,7},{7,6},{8,9},{9,8},{10,11... | collective-permute-start | bytes 3145736 | tf_op jit(solution)/shard_map/ppermute | solution.py:485
  32.8 6.2 %collective-permute-start.6 = (bf16[4,256,256]{2,1,0:T(8,128)(2,1)S(1)}, bf16[4,256,256]{2,1,0:T(8,128)(2,1)S(1)}, u32[]{:S(2)}, u32[]{:S(2)}) collective-permute-start(bf16[4,256,256]{2,1,0:T(8,128)(2,1)S(1)} %pad_maximum_fusion), channel_id=1, source_target_pairs={{0,1},{1,0},{2,3},{3,2},{4,5},{5,4},{6,7},{7,6},{8,9},{9,8},{10,11... | collective-permute-start | bytes 1572872 | tf_op jit(solution)/shard_map/ppermute | solution.py:518
  32.8 31.8 %collective-permute-start.9 = (bf16[4,256,256]{2,1,0:T(8,128)(2,1)}, bf16[4,256,256]{2,1,0:T(8,128)(2,1)S(1)}, u32[]{:S(2)}, u32[]{:S(2)}) collective-permute-start(bf16[4,256,256]{2,1,0:T(8,128)(2,1)} %get-tuple-element.37), channel_id=1, source_target_pairs={{0,2},{2,4},{4,6},{6,8},{8,10},{10,12},{12,14},{14,0},{1,3},{3,5},... | collective-permute-start | bytes 1572872 | tf_op jit(solution)/shard_map/ppermute | solution.py:499
  34.0 30.6 %collective-permute-start.10 = (bf16[4,256,256]{2,1,0:T(8,128)(2,1)}, bf16[4,256,256]{2,1,0:T(8,128)(2,1)}, u32[]{:S(2)}, u32[]{:S(2)}) collective-permute-start(bf16[4,256,256]{2,1,0:T(8,128)(2,1)} %get-tuple-element.31), channel_id=1, source_target_pairs={{2,0},{4,2},{6,4},{8,6},{10,8},{12,10},{14,12},{0,14},{3,1},{5,3},... | collective-permute-start | bytes 1572872 | tf_op jit(solution)/shard_map/ppermute | solution.py:498
  48.9 6.4 %copy-start.8 = (s32[4,64,2]{1,2,0:T(2,128)S(1)}, s32[4,64,2]{1,2,0:T(2,128)}, u32[]{:S(2)}) copy-start(s32[4,64,2]{1,2,0:T(2,128)} %param.20) | copy-start | bytes 6148
  48.9 6.4 %copy-start.11 = (s32[4,64]{1,0:T(4,128)S(1)}, s32[4,64]{1,0:T(4,128)}, u32[]{:S(2)}) copy-start(s32[4,64]{1,0:T(4,128)} %mask.1) | copy-start | bytes 3076
  48.9 9.4 %copy-start.2 = (f32[17,256,256]{2,1,0:T(8,128)S(1)}, f32[17,256,256]{2,1,0:T(8,128)}, u32[]{:S(2)}) copy-start(f32[17,256,256]{2,1,0:T(8,128)} %near.1.near_total) | copy-start | bytes 13369348
  49.0 9.3 %collective-permute-start.8 = (bf16[512,256]{1,0:T(8,128)(2,1)S(1)}, bf16[512,256]{1,0:T(8,128)(2,1)S(1)}, u32[]{:S(2)}, u32[]{:S(2)}) collective-permute-start(bf16[512,256]{1,0:T(8,128)(2,1)S(1)} %get-tuple-element.39), channel_id=1, source_target_pairs={{0,1},{1,0},{2,3},{3,2},{4,5},{5,4},{6,7},{7,6},{8,9},{9,8},{10,11... | collective-permute-start | bytes 786440 | tf_op jit(solution)/shard_map/ppermute | solution.py:537
  53.7 4.6 %collective-permute-start.7 = (bf16[512,256]{1,0:T(8,128)(2,1)S(1)}, bf16[512,256]{1,0:T(8,128)(2,1)S(1)}, u32[]{:S(2)}, u32[]{:S(2)}) collective-permute-start(bf16[512,256]{1,0:T(8,128)(2,1)S(1)} %get-tuple-element.40), channel_id=1, source_target_pairs={{0,1},{1,0},{2,3},{3,2},{4,5},{5,4},{6,7},{7,6},{8,9},{9,8},{10,11... | collective-permute-start | bytes 786440 | tf_op jit(solution)/shard_map/ppermute | solution.py:536
